TPU v7x, 128 devices: a whole 4x4x4 slice. The times are simulated.
128 devices in a mesh: ctx: 8 (over x, y_lo), exp: 16 (over y_hi, z, core).
Axes of the slice: x: 4, y: 4 (y_hi: 2, y_lo: 2; y = y_hi * 2 + y_lo), z: 4, core: 2. Of those that a mesh axis runs over, the one named last changes fastest.
Arguments:
- queries: bfloat16 [2048, 4096], P('ctx', 'exp'), may hold values from -4.5 to 4.5, as said below
- keys: bfloat16 [2048, 512], P('ctx'), may hold values from -4.5 to 4.5, as said below
- values: bfloat16 [2048, 512], P('ctx'), may hold values from -6 to 6
- out_proj: bfloat16 [4096, 4096], P('exp'), may hold values from -0.5 to 0.5
- residual: bfloat16 [2048, 4096], P(('ctx', 'exp')), may hold values from -3 to 3
- norm_gain: float32 [4096], replicated, may hold values from 0.5 to 1.5
- routes: int32 [2048, 8], P(('ctx', 'exp')), may hold values from 0 to 127, all different within a row; in each aligned block of 16 rows (0 to 15, 16 to 31, ...) at most 2 rows name the same one
- route_weights: float32 [2048, 8], P(('ctx', 'exp')), may hold values from 0.2 to 1
- w_gate: bfloat16 [128, 4096, 768], P(('ctx', 'exp')), may hold values from -0.09375 to 0.09375
- w_up: bfloat16 [128, 4096, 768], P(('ctx', 'exp')), may hold values from -0.09375 to 0.09375
- w_down: bfloat16 [128, 768, 4096], P(('ctx', 'exp')), may hold values from -0.21875 to 0.21875
Outputs:
- hidden_state: bfloat16 [2048, 4096], P(('ctx', 'exp'))
- expert_mix: float32 [2048, 4096], P(('ctx', 'exp'))
Inputs may be any that keep to these rules, and one draw needn't show every extreme that they name: Entries of queries are real values within the range. Entries of keys are real values within the range. `routes`: each token names 8 different experts; the 16 tokens of one device (aligned blocks of rows) name any one expert at most 2 times, a bound that some block reaches.
All inputs are finite; a program needn't handle non-finite values.
Results may differ from a plain program's by a relative error of at most 0.03.
Values may be sent and summed in bfloat16 or wider, within the bound.
No kernel may reach another device: no remote copies, remote signals or barrier semaphores. Data moves between devices by JAX's collectives and lax.ppermute only.
A program may use at most 128 MiB of HBM per device.

v0:
```python
import math

import jax
import jax.numpy as jnp
from jax import lax
from jax.sharding import PartitionSpec as P

D = 4096
QUERY_HEADS = 32
KEY_VALUE_HEADS = 4
HEAD_WIDTH = 128
TOP = 8


def expert_rows(row_block, gate_matrix, up_matrix, down_matrix):
    gate = jnp.dot(row_block, gate_matrix, preferred_element_type=jnp.float32)
    upward = jnp.dot(row_block, up_matrix, preferred_element_type=jnp.float32)
    active = (jax.nn.silu(gate) * upward).astype(jnp.bfloat16)
    return jnp.dot(active, down_matrix, preferred_element_type=jnp.float32).astype(jnp.bfloat16)


def attend_block(state, query_block, key_rows, value_rows, first_row, inv_root):
    old_max, old_sum, old_acc = state
    piece_rows = key_rows.shape[0]
    block_rows = query_block.shape[1]
    scores = (
        jnp.einsum("hqd,kd->hqk", query_block, key_rows, preferred_element_type=jnp.float32)
        * inv_root
    )
    query_pos = first_row + lax.iota(jnp.int32, block_rows)
    key_pos = lax.iota(jnp.int32, piece_rows)
    visible = (key_pos[None, :] <= query_pos[:, None])[None]
    row_max = jnp.max(jnp.where(visible, scores, -1e30), axis=-1)
    new_max = jnp.maximum(old_max, row_max)
    weights = jnp.where(visible, jnp.exp(scores - new_max[..., None]), 0.0)
    new_sum = jnp.sum(weights, axis=-1)
    product = jnp.einsum(
        "hqk,kd->hqd", weights.astype(jnp.bfloat16), value_rows, preferred_element_type=jnp.float32
    )
    return (new_max, new_sum, product)


def on_device(
    queries,
    keys,
    values,
    out_proj,
    residual,
    norm_gain,
    routes,
    route_weights,
    w_gate,
    w_up,
    w_down,
):
    seq_local = queries.shape[0]
    local_heads = queries.shape[1] // HEAD_WIDTH
    heads_per_group = QUERY_HEADS // KEY_VALUE_HEADS
    ctx_index = lax.axis_index("ctx")
    exp_index = lax.axis_index("exp")
    ctx_count = lax.axis_size("ctx")
    exp_count = lax.axis_size("exp")
    shared_head = exp_index * local_heads // heads_per_group
    own_keys = lax.dynamic_slice_in_dim(keys, shared_head * HEAD_WIDTH, HEAD_WIDTH, 1)
    own_values = lax.dynamic_slice_in_dim(values, shared_head * HEAD_WIDTH, HEAD_WIDTH, 1)
    query_heads = queries.reshape(seq_local, local_heads, HEAD_WIDTH).transpose(1, 0, 2)
    block_rows = min(512, seq_local)
    first_token = ctx_index * seq_local
    inv_root = 1.0 / math.sqrt(HEAD_WIDTH)
    key_rows = lax.all_gather(own_keys, "ctx", axis=0, tiled=True)
    value_rows = lax.all_gather(own_values, "ctx", axis=0, tiled=True)
    max_all = jnp.full((local_heads, seq_local), -1e30, jnp.float32)
    sum_all = jnp.zeros((local_heads, seq_local), jnp.float32)
    acc_all = jnp.zeros((local_heads, seq_local, HEAD_WIDTH), jnp.float32)
    first_row = first_token + 0
    state = (max_all, sum_all, acc_all)
    state = lax.cond(
        jnp.int32(0) <= first_row + block_rows - 1,
        lambda inner: attend_block(inner, query_heads, key_rows, value_rows, first_row, inv_root),
        lambda inner: inner,
        state,
    )
    results = [state]
    sum_all = jnp.concatenate([member[1] for member in results], axis=1)
    acc_all = jnp.concatenate([member[2] for member in results], axis=1)
    attended = (acc_all / sum_all[..., None]).astype(jnp.bfloat16)
    attended = attended.transpose(1, 0, 2).reshape(seq_local, local_heads * HEAD_WIDTH)
    projected = lax.psum_scatter(
        jnp.dot(attended, out_proj, preferred_element_type=jnp.float32).astype(jnp.bfloat16),
        "exp",
        scatter_dimension=0,
        tiled=True,
    ).astype(jnp.float32)
    hidden_state = (residual.astype(jnp.float32) + projected).astype(jnp.bfloat16)
    widened = hidden_state.astype(jnp.float32)
    normed = (
        widened * lax.rsqrt(jnp.mean(widened * widened, axis=-1, keepdims=True) + 1e-06) * norm_gain
    ).astype(jnp.bfloat16)
    tokens_local = residual.shape[0]
    expert_count = ctx_count * exp_count
    capacity = max(2, 2 * tokens_local * TOP // expert_count)
    flat_routes = routes.reshape(-1)
    one_hot = (flat_routes[:, None] == lax.iota(jnp.int32, expert_count)[None, :]).astype(jnp.int32)
    ranks = jnp.sum(jnp.cumsum(one_hot, axis=0) * one_hot, axis=1) - 1
    slots = flat_routes * capacity + ranks
    tallies = jnp.sum(one_hot, axis=0)
    token_of = lax.iota(jnp.int32, tokens_local * TOP) // TOP
    outgoing = jnp.zeros((expert_count * capacity, D), jnp.bfloat16).at[slots].set(normed[token_of])
    outgoing = outgoing.reshape(expert_count, capacity, D)
    incoming, arrived = (
        lax.all_to_all(outgoing, ("ctx", "exp"), split_axis=0, concat_axis=0, tiled=True),
        lax.all_to_all(tallies, ("ctx", "exp"), split_axis=0, concat_axis=0, tiled=True),
    )
    live = lax.iota(jnp.int32, capacity)[None, :] < arrived[:, None]
    flat_rows = incoming.reshape(-1, D)
    flat_live = live.reshape(-1)
    gate_matrix = w_gate[0]
    up_matrix = w_up[0]
    down_matrix = w_down[0]
    produced = expert_rows(flat_rows, gate_matrix, up_matrix, down_matrix)
    produced = jnp.where(flat_live[:, None], produced, jnp.zeros((), jnp.bfloat16))
    returning = produced.reshape(expert_count, capacity, D)
    returned = lax.all_to_all(returning, ("ctx", "exp"), split_axis=0, concat_axis=0, tiled=True)
    picked = returned.reshape(-1, D)[slots].reshape(tokens_local, TOP, D)
    expert_mix = jnp.sum(route_weights[..., None] * picked.astype(jnp.float32), axis=1)
    return (hidden_state, expert_mix)


def solution(mesh):
    placed = (
        P("ctx", "exp"),
        P("ctx", None),
        P("ctx", None),
        P("exp", None),
        P(("ctx", "exp"), None),
        P(),
        P(("ctx", "exp"), None),
        P(("ctx", "exp"), None),
        P(("ctx", "exp"), None, None),
        P(("ctx", "exp"), None, None),
        P(("ctx", "exp"), None, None),
    )
    return jax.shard_map(
        on_device,
        mesh=mesh,
        in_specs=placed,
        out_specs=(P(("ctx", "exp"), None), P(("ctx", "exp"), None)),
        check_vma=False,
    )
```

profile of v0, /device:TPU:1, one launch (start us, length us, event | category | flops | bytes accessed | tf_op | source)
XLA Modules:
  0.0 274.8 jit_solution(17191745859682291516)
XLA Ops:
  7.2 0.0 copy-start
  7.2 0.0 reduce-scatter.2.cloned.1.call-start
  7.2 1.0 constant_dynamic-slice_fusion.1
  8.2 24.3 %all_gather.6 = bf16[2048,128]{1,0:T(8,128)(2,1)S(1)} all-gather(bf16[256,128]{1,0:T(8,128)(2,1)S(1)} %constant_dynamic-slice_fusion.1), channel_id=1, replica_groups=mesh['ctx'=8,'exp'=16] {'ctx'}, dimensions={0}, use_global_device_ids=true | all-gather | bytes 589824 | tf_op jit(solution)/shard_map/all_gather | solution.py:70
  32.6 0.8 constant_dynamic-slice_fusion
  33.4 23.1 %all_gather.7 = bf16[2048,128]{1,0:T(8,128)(2,1)S(1)} all-gather(bf16[256,128]{1,0:T(8,128)(2,1)S(1)} %constant_dynamic-slice_fusion), channel_id=1, replica_groups=mesh['ctx'=8,'exp'=16] {'ctx'}, dimensions={0}, use_global_device_ids=true | all-gather | bytes 589824 | tf_op jit(solution)/shard_map/all_gather | solution.py:71
  56.5 1.0 copy.29
  57.5 3.9 %conditional.1 = (f32[2,256]{1,0:T(2,128)S(1)}, f32[2,256,128]{1,2,0:T(8,128)S(1)}) conditional(s32[]{:T(128)} %convert_element_type.43, () %tuple.16, (s32[]{:T(128)}, bf16[2,256,128]{1,2,0:T(8,128)(2,1)S(1)}, bf16[2048,128]{1,0:T(8,128)(2,1)S(1)}, bf16[2048,128]{1,0:T(8,128)(2,1)S(1)}) %tuple.31), branch_computations={%region_0.1_spmd, %region_1.4_spmd} | conditional | flops 548929280 | bytes 16136212 | solution.py:77
  57.6 0.4 iota_compare_fusion
  57.9 1.1 select_reduce_fusion
  59.1 1.1 fusion.2
  60.2 1.3 fusion.1
  61.5 0.0 copy-start.4
  61.5 0.0 copy-start.2
  61.5 0.0 copy-start.3
  61.6 0.0 copy-done
  61.6 2.1 convolution_convert_fusion
  63.7 0.0 reduce-scatter.2.cloned.1.call-update
  63.7 0.0 copy-done.4
  63.7 0.1 copy.33
  63.8 0.1 eq.15
  63.9 0.1 fusion.43
  64.0 0.2 reduce_window_sum.11
  64.1 0.2 select_reduce_fusion.1
  64.3 0.7 copy.34
  65.0 22.1 %all-to-all-start = ((s32[128,1,1]{2,1,0:T(1,128)}), s32[128,1,1]{2,1,0:T(1,128)S(1)}, u32[]{:S(2)}, u32[]{:S(2)}) async-start(s32[128,1,1]{2,1,0:T(1,128)} %copy.34), calls=%async_computation.1 | async-start | bytes 131072 | tf_op jit(solution)/shard_map/all_to_all | solution.py:112
  87.1 0.1 copy.35
  87.2 0.1 mul.72
  87.3 59.6 %reduce-scatter.2.cloned.1.call-done = bf16[16,4096]{1,0:T(8,128)(2,1)} async-done(((bf16[256,4096]{1,0:T(8,128)(2,1)}), bf16[16,4096]{1,0:T(8,128)(2,1)}) %reduce-scatter.2.cloned.1.call-update) | async-done | bytes 131088 | tf_op jit(solution)/shard_map/reduce_scatter | solution.py:88
  146.9 0.0 copy-done.2
  146.9 1.1 fusion.40
  148.0 0.0 copy-start.1
  148.0 0.0 copy-done.3
  148.0 0.1 fusion.42
  148.1 6.7 %scatter_custom_fusion = bf16[256,4096]{1,0:T(8,128)(2,1)} fusion(s32[128]{0:T(128)S(1)} %fusion.46, bf16[16,4096]{1,0:T(8,128)(2,1)S(1)} %fusion.42, s32[1024]{0:T(1024)S(1)} %pad_clamp_fusion.1, bf16[]{:T(256)} %constant.79.clone.1), kind=kCustom, calls=%fused_computation.30 | custom fusion | bytes 2097154 | tf_op jit(solution)/shard_map/scatter | solution.py:108
  154.8 4.4 %reshape.160 = bf16[128,2,4096]{2,1,0:T(2,128)(2,1)} reshape(bf16[256,4096]{1,0:T(8,128)(2,1)} %scatter_custom_fusion) | data formatting | bytes 4194304 | tf_op jit(solution)/shard_map/reshape | solution.py:109
  159.2 0.0 all-to-all-done
  159.2 0.0 copy-done.1
  159.2 9.5 %all-to-all-start.1 = ((bf16[128,2,4096]{2,1,0:T(2,128)(2,1)}), bf16[128,2,4096]{2,1,0:T(2,128)(2,1)}, u32[]{:S(2)}, u32[]{:S(2)}) async-start(bf16[128,2,4096]{2,1,0:T(2,128)(2,1)} %reshape.160), calls=%async_computation.2 | async-start | bytes 4194304 | tf_op jit(solution)/shard_map/all_to_all | solution.py:111
  168.7 2.4 reduce
  171.1 0.1 iota_compare_fusion.2
  171.2 0.1 lt.52
  171.3 26.8 %all-to-all-done.1 = bf16[128,2,4096]{2,1,0:T(2,128)(2,1)} async-done(((bf16[128,2,4096]{2,1,0:T(2,128)(2,1)}), bf16[128,2,4096]{2,1,0:T(2,128)(2,1)}, u32[]{:S(2)}, u32[]{:S(2)}) %all-to-all-start.1) | async-done | bytes 2097184 | tf_op jit(solution)/shard_map/all_to_all | solution.py:111
  198.1 4.1 %reshape.161 = bf16[256,4096]{1,0:T(8,128)(2,1)} reshape(bf16[128,2,4096]{2,1,0:T(2,128)(2,1)} %all-to-all-done.1) | data formatting | bytes 4194304 | tf_op jit(solution)/shard_map/reshape | solution.py:115
  202.2 5.2 %fusion.14 = f32[256,768]{1,0:T(8,128)S(1)} fusion(bf16[256,4096]{1,0:T(8,128)(2,1)} %reshape.161, bf16[1,4096,768]{2,1,0:T(8,128)(2,1)} %param.21), kind=kOutput, calls=%fused_computation.21 | convolution fusion | flops 1610612736 | bytes 9175040 | tf_op jit(solution)/shard_map/dot_general | solution.py:16
  207.4 11.1 %fusion.19 = bf16[256,4096]{1,0:T(8,128)(2,1)} fusion(bf16[1,768,4096]{2,1,0:T(8,128)(2,1)} %param.23, pred[256]{0:T(512)(128)(4,1)S(1)} %lt.52, bf16[256,4096]{1,0:T(8,128)(2,1)} %reshape.161, bf16[1,4096,768]{2,1,0:T(8,128)(2,1)} %param.22, f32[256,768]{1,0:T(8,128)S(1)} %fusion.14), kind=kOutput, calls=%fused_computation.25 | convolution fusion | flops 3224502272 | bytes 17563904 | tf_op jit(solution)/shard_map/dot_general | solution.py:19
  218.6 0.0 copy-start.5
  218.6 4.4 %reshape.162 = bf16[128,2,4096]{2,1,0:T(2,128)(2,1)} reshape(bf16[256,4096]{1,0:T(8,128)(2,1)} %fusion.19) | data formatting | bytes 4194304 | tf_op jit(solution)/shard_map/reshape | solution.py:122
  223.0 5.8 %all-to-all-start.2 = ((bf16[128,2,4096]{2,1,0:T(2,128)(2,1)}), bf16[128,2,4096]{2,1,0:T(2,128)(2,1)}, u32[]{:S(2)}, u32[]{:S(2)}) async-start(bf16[128,2,4096]{2,1,0:T(2,128)(2,1)} %reshape.162), calls=%async_computation.3 | async-start | bytes 4194304 | tf_op jit(solution)/shard_map/all_to_all | solution.py:123
  228.8 0.0 copy-done.5
  228.8 0.1 copy.32
  228.9 29.4 %all-to-all-done.2 = bf16[128,2,4096]{2,1,0:T(2,128)(2,1)} async-done(((bf16[128,2,4096]{2,1,0:T(2,128)(2,1)}), bf16[128,2,4096]{2,1,0:T(2,128)(2,1)}, u32[]{:S(2)}, u32[]{:S(2)}) %all-to-all-start.2) | async-done | bytes 2097184 | tf_op jit(solution)/shard_map/all_to_all | solution.py:123
  258.3 4.1 %reshape.163 = bf16[256,4096]{1,0:T(8,128)(2,1)} reshape(bf16[128,2,4096]{2,1,0:T(2,128)(2,1)} %all-to-all-done.2) | data formatting | bytes 4194304 | tf_op jit(solution)/shard_map/reshape | solution.py:124
  262.4 4.1 %gather_fusion = bf16[128,4096]{1,0:T(8,128)(2,1)S(1)} fusion(bf16[256,4096]{1,0:T(8,128)(2,1)} %reshape.163, s32[1024]{0:T(1024)S(1)} %pad_clamp_fusion), kind=kCustom, calls=%fused_computation.1 | custom fusion | bytes 2097664 | tf_op jit(solution)/shard_map/gather | solution.py:124
  266.5 1.5 fusion.22
  (9 shorter events, 0.1 us)
Async XLA Ops:
  7.2 54.4 %copy-start = (bf16[256,4096]{1,0:T(8,128)(2,1)S(1)}, bf16[256,4096]{1,0:T(8,128)(2,1)}, u32[]{:S(2)}) copy-start(bf16[256,4096]{1,0:T(8,128)(2,1)} %param.16) | copy-start | bytes 6291460
  7.2 139.7 %reduce-scatter.2.cloned.1.call-start = ((), (), s32[]{:S(2)}) async-start(), calls=%async_computation.4 | async-start | bytes 2228224 | tf_op jit(solution)/shard_map/reduce_scatter | solution.py:88
  61.5 2.2 copy-start.4
  61.5 85.4 %copy-start.2 = (bf16[16,4096]{1,0:T(8,128)(2,1)S(1)}, bf16[16,4096]{1,0:T(8,128)(2,1)}, u32[]{:S(2)}) copy-start(bf16[16,4096]{1,0:T(8,128)(2,1)} %param.17) | copy-start | bytes 393220
  61.5 86.5 %copy-start.3 = (f32[4096]{0:T(1024)S(1)}, f32[4096]{0:T(1024)}, u32[]{:S(2)}) copy-start(f32[4096]{0:T(1024)} %param.18) | copy-start | bytes 49156
  65.0 94.1 %all-to-all-start = ((s32[128,1,1]{2,1,0:T(1,128)}), s32[128,1,1]{2,1,0:T(1,128)S(1)}, u32[]{:S(2)}, u32[]{:S(2)}) async-start(s32[128,1,1]{2,1,0:T(1,128)} %copy.34), calls=%async_computation.1 | async-start | bytes 131072 | tf_op jit(solution)/shard_map/all_to_all | solution.py:112
  148.0 11.2 %copy-start.1 = (bf16[16,4096]{1,0:T(8,128)(2,1)}, bf16[16,4096]{1,0:T(8,128)(2,1)S(1)}, u32[]{:S(2)}) copy-start(bf16[16,4096]{1,0:T(8,128)(2,1)S(1)} %get-tuple-element.34) | copy-start | bytes 393220
  159.2 38.9 %all-to-all-start.1 = ((bf16[128,2,4096]{2,1,0:T(2,128)(2,1)}), bf16[128,2,4096]{2,1,0:T(2,128)(2,1)}, u32[]{:S(2)}, u32[]{:S(2)}) async-start(bf16[128,2,4096]{2,1,0:T(2,128)(2,1)} %reshape.160), calls=%async_computation.2 | async-start | bytes 4194304 | tf_op jit(solution)/shard_map/all_to_all | solution.py:111
  218.6 10.2 %copy-start.5 = (f32[16,8]{0,1:T(8,128)S(1)}, f32[16,8]{0,1:T(8,128)}, u32[]{:S(2)}) copy-start(f32[16,8]{0,1:T(8,128)} %param.20) | copy-start | bytes 1540
  223.0 35.3 %all-to-all-start.2 = ((bf16[128,2,4096]{2,1,0:T(2,128)(2,1)}), bf16[128,2,4096]{2,1,0:T(2,128)(2,1)}, u32[]{:S(2)}, u32[]{:S(2)}) async-start(bf16[128,2,4096]{2,1,0:T(2,128)(2,1)} %reshape.162), calls=%async_computation.3 | async-start | bytes 4194304 | tf_op jit(solution)/shard_map/all_to_all | solution.py:123
Sparse Core Ops, SparseCore 0:
  63.8 83.0 reduce-scatter.1
where the time goes:
time: 276 us; the launch traced here: 275 us
  waiting for transfers between devices  116 us (42%)
  blocking collectives  47.5 us (17%)
  starting transfers between devices  37.4 us (14%)
  local copies, waits for them, and re-layouts  32 us (12%)
  matrix products  20.7 us (8%)
  between operations  14.2 us (5%)
  other arithmetic  7.24 us (3%)
    reduce_scatter x1, waiting for transfers between devices, on_device(): lax.psum_scatter(jnp.dot(attended, out_proj, preferred_element_type=jnp.f...  59.6 us
    all_to_all x1, waiting for transfers between devices, on_device(): lax.all_to_all(returning, ('ctx', 'exp'), split_axis=0, concat_axis=0, ti...  29.4 us
    all_to_all x1, waiting for transfers between devices, on_device(): lax.all_to_all(outgoing, ('ctx', 'exp'), split_axis=0, concat_axis=0, til...  26.8 us
    all_gather x1, blocking collectives, on_device(): key_rows = lax.all_gather(own_keys, 'ctx', axis=0, tiled=True)  24.3 us
    all_gather x1, blocking collectives, on_device(): value_rows = lax.all_gather(own_values, 'ctx', axis=0, tiled=True)  23.1 us
    all_to_all x1, starting transfers between devices, on_device(): lax.all_to_all(tallies, ('ctx', 'exp'), split_axis=0, concat_axis=0, tile...  22.1 us
    dot_general x1, matrix products, expert_rows(): jnp.dot(active, down_matrix, preferred_element_type=jnp.float32)  11.1 us
    all_to_all x1, starting transfers between devices, on_device(): lax.all_to_all(outgoing, ('ctx', 'exp'), split_axis=0, concat_axis=0, til...  9.53 us
  transfers between devices with their start and end apart: 4, of which 3 were waited for; matrix products, arithmetic and copies ran while one was open for 6% of the time, Pallas kernels for 0%

commit v1 on v0

v1 whole, which is shorter than its diff:
```python
import math

import jax
import jax.numpy as jnp
from jax import lax
from jax.experimental import pallas as pl
from jax.experimental.pallas import tpu as pltpu
from jax.sharding import Mesh
from jax.sharding import PartitionSpec as P

D = 4096
HEAD_WIDTH = 128
TOP = 8
TOKENS = 16
EXPERTS = 128
CAP = 2
SLOTS = EXPERTS * CAP
BLOCK = 256
FF = 768
PIECES = D // 128
CTX = ("x", "yl")
CHIPS = ("yh", "z")
ALL = ("x", "yl", "yh", "z", "c")
INV_ROOT = 1.0 / math.sqrt(HEAD_WIDTH)
MIB = 1 << 20

VMEM = pl.BlockSpec(memory_space=pltpu.VMEM)
SMEM = pl.BlockSpec(memory_space=pltpu.SMEM)
HBM = pl.BlockSpec(memory_space=pl.ANY)


def attention_kernel(
    place, own_queries, twin_queries, blocks, own_proj, twin_proj, out, w_buf, sems, m_ref, l_ref, acc
):
    copies = [
        pltpu.make_async_copy(own_proj, w_buf.at[pl.ds(0, 256)], sems.at[0]),
        pltpu.make_async_copy(twin_proj, w_buf.at[pl.ds(256, 256)], sems.at[1]),
    ]
    for copy in copies:
        copy.start()
    own_block = place[0]
    core = place[1]
    stacked = jnp.concatenate(
        [
            own_queries[:, 0:128],
            own_queries[:, 128:256],
            twin_queries[:, 0:128],
            twin_queries[:, 128:256],
        ],
        axis=0,
    )

    def scores_of(block):
        return (
            lax.dot_general(
                stacked,
                blocks[block, :, 0:128],
                (((1,), (1,)), ((), ())),
                preferred_element_type=jnp.float32,
            )
            * INV_ROOT
        )

    row = lax.broadcasted_iota(jnp.int32, (512, BLOCK), 0) % 128
    position = (row // TOKENS) * (2 * TOKENS) + core * TOKENS + row % TOKENS
    visible = lax.broadcasted_iota(jnp.int32, (512, BLOCK), 1) <= position
    scores = jnp.where(visible, scores_of(own_block), -1e30)
    row_max = jnp.max(scores, axis=1, keepdims=True)
    probs = jnp.exp(scores - row_max)
    m_ref[...] = jnp.broadcast_to(row_max, (512, 128))
    l_ref[...] = jnp.broadcast_to(jnp.sum(probs, axis=1, keepdims=True), (512, 128))
    acc[...] = jnp.dot(
        probs.astype(jnp.bfloat16),
        blocks[own_block, :, 128:256],
        preferred_element_type=jnp.float32,
    )

    @pl.loop(0, own_block)
    def earlier(block):
        scores = scores_of(block)
        old_max = m_ref[:, 0:1]
        new_max = jnp.maximum(old_max, jnp.max(scores, axis=1, keepdims=True))
        shrink = jnp.exp(old_max - new_max)
        probs = jnp.exp(scores - new_max)
        m_ref[...] = jnp.broadcast_to(new_max, (512, 128))
        l_ref[...] = l_ref[...] * shrink + jnp.sum(probs, axis=1, keepdims=True)
        acc[...] = acc[...] * shrink + jnp.dot(
            probs.astype(jnp.bfloat16),
            blocks[block, :, 128:256],
            preferred_element_type=jnp.float32,
        )

    attended = (acc[...] / l_ref[...]).astype(jnp.bfloat16)
    wide = jnp.concatenate([attended[h * 128 : (h + 1) * 128] for h in range(4)], axis=1)
    for copy in copies:
        copy.wait()

    for piece in range(D // 512):
        columns = slice(piece * 512, (piece + 1) * 512)
        out[:, columns] = jnp.dot(
            wide, w_buf[:, columns], preferred_element_type=jnp.float32
        ).astype(jnp.bfloat16)


def slots_kernel(routes, slots, counts):
    @pl.loop(0, EXPERTS)
    def clear(expert):
        counts[expert] = 0

    @pl.loop(0, TOKENS)
    def number(token):
        for choice in range(TOP):
            expert = routes[token, choice]
            rank = counts[expert]
            counts[expert] = rank + 1
            slots[token, choice] = expert * CAP + rank


def norm_kernel(slots, shares, residual, gain, hidden, outgoing, rows):
    total = residual[...].astype(jnp.float32)
    for share in range(8):
        total = total + shares[share].astype(jnp.float32)
    state = total.astype(jnp.bfloat16)
    hidden[...] = state
    wide = state.astype(jnp.float32)
    scale = lax.rsqrt(jnp.mean(wide * wide, axis=1, keepdims=True) + 1e-6)
    normed = wide * scale * gain[...]
    for piece in range(PIECES):
        rows[pl.ds(piece, TOKENS, stride=PIECES), :] = normed[:, piece * 128 : (piece + 1) * 128]

    @pl.loop(0, SLOTS // 8)
    def clear(group):
        outgoing[pl.ds(group * 8, 8)] = jnp.zeros((8, PIECES, 128), jnp.bfloat16)

    @pl.loop(0, TOKENS)
    def place(token):
        row = rows[pl.ds(pl.multiple_of(token * PIECES, PIECES), PIECES), :].astype(jnp.bfloat16)
        for choice in range(TOP):
            outgoing[slots[token, choice]] = row


def expert_kernel(incoming, w_gate, w_up, w_down, out, gate_buf, up_buf, down_buf, sems, wide, rows):
    def fetch(source, target, index):
        copy = pltpu.make_async_copy(source, target, sems.at[index])
        copy.start()
        return copy

    gates, ups, downs = [], [], []
    for part in range(3):
        columns = pl.ds(part * 256, 256)
        gates.append(fetch(w_gate.at[0, :, columns], gate_buf.at[part], part))
        ups.append(fetch(w_up.at[0, :, columns], up_buf.at[part], 3 + part))
    for part in range(4):
        columns = pl.ds(part * 1024, 1024)
        downs.append(fetch(w_down.at[0, :, columns], down_buf.at[part], 6 + part))

    @pl.loop(0, SLOTS // 32)
    def widen(group):
        wide[pl.ds(group * 32 * PIECES, 32 * PIECES), :] = incoming[
            pl.ds(group * 32 * PIECES, 32 * PIECES), :
        ].astype(jnp.float32)

    for piece in range(PIECES):
        rows[:, piece * 128 : (piece + 1) * 128] = wide[
            pl.ds(piece, SLOTS, stride=PIECES), :
        ].astype(jnp.bfloat16)
    actives = []
    for part in range(3):
        gates[part].wait()
        gate = jnp.dot(rows[...], gate_buf[part], preferred_element_type=jnp.float32)
        ups[part].wait()
        upward = jnp.dot(rows[...], up_buf[part], preferred_element_type=jnp.float32)
        actives.append((gate / (1.0 + jnp.exp(-gate)) * upward).astype(jnp.bfloat16))
    active = jnp.concatenate(actives, axis=1)
    for part in range(4):
        downs[part].wait()
        for half in range(2):
            produced = jnp.dot(
                active,
                down_buf[part, :, half * 512 : (half + 1) * 512],
                preferred_element_type=jnp.float32,
            )
            for lane in range(4):
                piece = part * 8 + half * 4 + lane
                wide[pl.ds(piece, SLOTS, stride=PIECES), :] = produced[
                    :, lane * 128 : (lane + 1) * 128
                ]

    @pl.loop(0, SLOTS // 32)
    def narrow(group):
        out[pl.ds(group * 32 * PIECES, 32 * PIECES), :] = wide[
            pl.ds(group * 32 * PIECES, 32 * PIECES), :
        ].astype(jnp.bfloat16)


def mix_kernel(slots, weights, returned, out, rows):
    @pl.loop(0, TOKENS)
    def gather(token):
        total = jnp.zeros((PIECES, 128), jnp.float32)
        for choice in range(TOP):
            total = total + weights[token, choice] * returned[slots[token, choice]].astype(
                jnp.float32
            )
        rows[pl.ds(pl.multiple_of(token * PIECES, PIECES), PIECES), :] = total

    for piece in range(PIECES):
        out[:, piece * 128 : (piece + 1) * 128] = rows[pl.ds(piece, TOKENS, stride=PIECES), :]


def swap_cores(array):
    return lax.ppermute(array, "c", [(0, 1), (1, 0)])


def gather_blocks(block):
    spread = jnp.broadcast_to(block[None], (8,) + block.shape)
    return lax.all_to_all(spread, CTX, split_axis=0, concat_axis=0, tiled=True)


def on_device(
    queries,
    keys,
    values,
    out_proj,
    residual,
    norm_gain,
    routes,
    route_weights,
    w_gate,
    w_up,
    w_down,
):
    ctx_index = lax.axis_index(CTX)
    core = lax.axis_index("c")
    shared_head = lax.axis_index(CHIPS) // 2
    own_keys = lax.dynamic_slice_in_dim(keys, shared_head * HEAD_WIDTH, HEAD_WIDTH, 1)
    own_values = lax.dynamic_slice_in_dim(values, shared_head * HEAD_WIDTH, HEAD_WIDTH, 1)
    blocks = gather_blocks(jnp.concatenate([own_keys, own_values], axis=1))
    split = queries.reshape(8, 2, TOKENS, 256)
    own_queries = lax.dynamic_index_in_dim(split, core, 1, False).reshape(128, 256)
    sent_queries = lax.dynamic_index_in_dim(split, 1 - core, 1, False).reshape(128, 256)
    twin_queries = swap_cores(sent_queries)
    twin_proj = swap_cores(out_proj)

    slots = pl.pallas_call(
        slots_kernel,
        out_shape=jax.ShapeDtypeStruct((TOKENS, TOP), jnp.int32),
        in_specs=[SMEM],
        out_specs=SMEM,
        scratch_shapes=[pltpu.SMEM((EXPERTS,), jnp.int32)],
        name="number_slots",
    )(routes)

    place = jnp.stack([ctx_index, core]).astype(jnp.int32)
    partial = pl.pallas_call(
        attention_kernel,
        out_shape=jax.ShapeDtypeStruct((128, D), jnp.bfloat16),
        in_specs=[SMEM, VMEM, VMEM, VMEM, HBM, HBM],
        out_specs=VMEM,
        scratch_shapes=[
            pltpu.VMEM((512, D), jnp.bfloat16),
            pltpu.SemaphoreType.DMA((2,)),
            pltpu.VMEM((512, 128), jnp.float32),
            pltpu.VMEM((512, 128), jnp.float32),
            pltpu.VMEM((512, 128), jnp.float32),
        ],
        compiler_params=pltpu.CompilerParams(vmem_limit_bytes=24 * MIB),
        name="attend_project",
    )(place, own_queries, twin_queries, blocks, out_proj, twin_proj)

    shares = lax.all_to_all(
        partial.reshape(8, TOKENS, D), CHIPS, split_axis=0, concat_axis=0, tiled=True
    )
    hidden_state, outgoing = pl.pallas_call(
        norm_kernel,
        out_shape=(
            jax.ShapeDtypeStruct((TOKENS, D), jnp.bfloat16),
            jax.ShapeDtypeStruct((SLOTS, PIECES, 128), jnp.bfloat16),
        ),
        in_specs=[SMEM, VMEM, VMEM, VMEM],
        out_specs=(VMEM, VMEM),
        scratch_shapes=[pltpu.VMEM((TOKENS * PIECES, 128), jnp.float32)],
        compiler_params=pltpu.CompilerParams(vmem_limit_bytes=16 * MIB),
        name="norm_dispatch",
    )(slots, shares, residual, norm_gain.reshape(1, D))

    incoming = lax.all_to_all(
        outgoing.reshape(EXPERTS, CAP * PIECES, 128), ALL, split_axis=0, concat_axis=0, tiled=True
    )
    produced = pl.pallas_call(
        expert_kernel,
        out_shape=jax.ShapeDtypeStruct((SLOTS * PIECES, 128), jnp.bfloat16),
        in_specs=[VMEM, HBM, HBM, HBM],
        out_specs=VMEM,
        scratch_shapes=[
            pltpu.VMEM((3, D, 256), jnp.bfloat16),
            pltpu.VMEM((3, D, 256), jnp.bfloat16),
            pltpu.VMEM((4, FF, 1024), jnp.bfloat16),
            pltpu.SemaphoreType.DMA((10,)),
            pltpu.VMEM((SLOTS * PIECES, 128), jnp.float32),
            pltpu.VMEM((SLOTS, D), jnp.bfloat16),
        ],
        compiler_params=pltpu.CompilerParams(vmem_limit_bytes=48 * MIB),
        name="expert_rows",
    )(incoming.reshape(SLOTS * PIECES, 128), w_gate, w_up, w_down)
    returned = lax.all_to_all(
        produced.reshape(EXPERTS, CAP * PIECES, 128), ALL, split_axis=0, concat_axis=0, tiled=True
    )
    expert_mix = pl.pallas_call(
        mix_kernel,
        out_shape=jax.ShapeDtypeStruct((TOKENS, D), jnp.float32),
        in_specs=[SMEM, SMEM, VMEM],
        out_specs=VMEM,
        scratch_shapes=[pltpu.VMEM((TOKENS * PIECES, 128), jnp.float32)],
        compiler_params=pltpu.CompilerParams(vmem_limit_bytes=16 * MIB),
        name="mix",
    )(slots, route_weights, returned.reshape(SLOTS, PIECES, 128))
    return (hidden_state, expert_mix)


def solution(mesh):
    fine = Mesh(mesh.devices.reshape(4, 2, 2, 4, 2), ALL)
    exp = ("yh", "z", "c")
    placed = (
        P(CTX, exp),
        P(CTX, None),
        P(CTX, None),
        P(exp, None),
        P(ALL, None),
        P(),
        P(ALL, None),
        P(ALL, None),
        P(ALL, None, None),
        P(ALL, None, None),
        P(ALL, None, None),
    )
    return jax.shard_map(
        on_device,
        mesh=fine,
        in_specs=placed,
        out_specs=(P(ALL, None), P(ALL, None)),
        check_vma=False,
    )
```

time: 276 us -> 150 us (0.54)
  waiting for transfers between devices: 116 us -> 55.2 us
  Pallas kernels: 0 us -> 27.6 us
  local copies, waits for them, and re-layouts: 32 us -> 4.74 us
  matrix products: 20.7 us -> 0 us
  starting transfers between devices: 37.4 us -> 19.6 us
  between operations: 14.2 us -> 0.76 us
  other arithmetic: 7.24 us -> 0.09 us
  blocking collectives: 47.5 us -> 41.9 us
    reduce_scatter x1 -> x0, waiting for transfers between devices: 59.6 us -> none  [on_device(): lax.psum_scatter(jnp.dot(attended, out_proj, preferred_element_type=jnp.f...]
    all_gather x2 -> x0, blocking collectives: 47.5 us -> none  [the longest x1 24.3 us: on_device(): key_rows = lax.all_gather(own_keys, 'ctx', axis=0, tiled=True)]
    all_to_all x0 -> x1, blocking collectives: none -> 41.9 us  [on_device(): lax.all_to_all(outgoing.reshape(EXPERTS, CAP * PIECES, 128), ALL, split_a...]
    pallas_call x0 -> x5, Pallas kernels: none -> 27.6 us  [the longest x1 16.3 us: on_device(): pl.pallas_call(expert_kernel, out_shape=jax.ShapeDtypeStruct((SLOTS * PIE...]
    all_to_all x3, starting transfers between devices: 37.4 us -> 17.6 us  [the longest x1 7.52 us: on_device(): lax.all_to_all(partial.reshape(8, TOKENS, D), CHIPS, split_axis=0, concat...]
    dot_general x4 -> x0, matrix products: 19.5 us -> none  [the longest x1 11.1 us: expert_rows(): jnp.dot(active, down_matrix, preferred_element_type=jnp.float32)]
    reshape x4 -> x0, local copies, waits for them, and re-layouts: 17.1 us -> none  [the longest x1 4.42 us: on_device(): returning = produced.reshape(expert_count, capacity, D)]
    scatter x1 -> x0, local copies, waits for them, and re-layouts: 6.7 us -> none  [on_device(): jnp.zeros((expert_count * capacity, D), jnp.bfloat16).at[slots]]
  transfers between devices with their start and end apart: 4 -> 5, of which waited for: 3 -> 4; matrix products, arithmetic and copies ran while one was open for 6% -> 2% of each run, Pallas kernels for 0% -> 2%
where the time goes in v1:
time: 150 us
  waiting for transfers between devices  55.2 us (37%)
  blocking collectives  41.9 us (28%)
  Pallas kernels  27.6 us (18%)
  starting transfers between devices  19.6 us (13%)
  local copies, waits for them, and re-layouts  4.74 us (3%)
    all_to_all x1, blocking collectives, on_device(): lax.all_to_all(outgoing.reshape(EXPERTS, CAP * PIECES, 128), ALL, split_a...  41.9 us
    all_to_all x1, waiting for transfers between devices, on_device(): lax.all_to_all(produced.reshape(EXPERTS, CAP * PIECES, 128), ALL, split_a...  29.7 us
    pallas_call x1, Pallas kernels, on_device(): pl.pallas_call(expert_kernel, out_shape=jax.ShapeDtypeStruct((SLOTS * PIE...  16.3 us
    all_to_all x1, waiting for transfers between devices, gather_blocks(): return lax.all_to_all(spread, CTX, split_axis=0, concat_axis=0, tiled=True)  14.7 us
    all_to_all x1, waiting for transfers between devices, on_device(): lax.all_to_all(partial.reshape(8, TOKENS, D), CHIPS, split_axis=0, concat...  9.97 us
    all_to_all x1, starting transfers between devices, on_device(): lax.all_to_all(partial.reshape(8, TOKENS, D), CHIPS, split_axis=0, concat...  7.52 us
    all_to_all x1, starting transfers between devices, gather_blocks(): return lax.all_to_all(spread, CTX, split_axis=0, concat_axis=0, tiled=True)  5.12 us
    all_to_all x1, starting transfers between devices, on_device(): lax.all_to_all(produced.reshape(EXPERTS, CAP * PIECES, 128), ALL, split_a...  4.92 us
  transfers between devices with their start and end apart: 5, of which 4 were waited for; matrix products, arithmetic and copies ran while one was open for 2% of the time, Pallas kernels for 2%

profile of v1, /device:TPU:1, one launch (start us, length us, event | category | flops | bytes accessed | tf_op | source)
XLA Modules:
  0.0 149.9 jit_solution(2900615561390830804)
XLA Ops:
  0.6 0.0 copy-start.1
  0.6 0.0 copy-start.6
  0.7 1.5 %collective-permute-start.1 = (bf16[256,4096]{1,0:T(8,128)(2,1)}, bf16[256,4096]{1,0:T(8,128)(2,1)}, u32[]{:S(2)}, u32[]{:S(2)}) collective-permute-start(bf16[256,4096]{1,0:T(8,128)(2,1)} %own_proj.1), channel_id=1, source_target_pairs={{0,1},{1,0},{2,3},{3,2},{4,5},{5,4},{6,7},{7,6},{8,9},{9,8},{10,11... | collective-permute-start | bytes 6291464 | tf_op jit(solution)/shard_map/ppermute | solution.py:211
  2.2 0.9 constant_dynamic-slice_fusion
  3.1 1.0 broadcast_in_dim.2
  4.1 5.1 %all-to-all-start = ((bf16[8,256,256]{2,1,0:T(8,128)(2,1)}), bf16[8,256,256]{2,1,0:T(8,128)(2,1)S(1)}, u32[]{:S(2)}, u32[]{:S(2)}) async-start(bf16[8,256,256]{2,1,0:T(8,128)(2,1)} %broadcast_in_dim.2), calls=%async_computation | async-start | bytes 2097152 | tf_op jit(solution)/shard_map/all_to_all | solution.py:216
  9.2 0.0 copy-done.6
  9.2 0.5 collective-permute-start
  9.8 0.1 pad_add_fusion.place
  9.9 0.8 collective-permute-done.twin_queries
  10.7 14.7 %all-to-all-done.blocks = bf16[8,256,256]{2,1,0:T(8,128)(2,1)S(1)} async-done(((bf16[8,256,256]{2,1,0:T(8,128)(2,1)}), bf16[8,256,256]{2,1,0:T(8,128)(2,1)S(1)}, u32[]{:S(2)}, u32[]{:S(2)}) %all-to-all-start) | async-done | bytes 1048608 | tf_op jit(solution)/shard_map/all_to_all | solution.py:216
  25.3 0.0 collective-permute-done.1.twin_proj
  25.3 0.0 copy-done.1
  25.3 4.1 %attend_project.1 = bf16[128,4096]{1,0:T(8,128)(2,1)} custom-call(s32[2]{0:T(128)S(1)} %pad_add_fusion.place, bf16[128,256]{1,0:T(8,128)(2,1)S(1)} %bitcast.19, bf16[128,256]{1,0:T(8,128)(2,1)S(1)} %collective-permute-done.twin_queries, bf16[8,256,256]{2,1,0:T(8,128)(2,1)S(1)} %all-to-all-done.blocks, bf16[256,4096]{1,0:T(8,128)(2,1)S(1)} %copy-done.1, ...), custom_call_target="tpu_custom_call" | custom-call | tf_op jit(solution)/shard_map/attend_project/pallas_call | solution.py:254
  29.5 0.0 copy-start.7
  29.5 0.0 copy-start.2
  29.5 0.0 copy-start.5
  29.5 7.5 %all-to-all-start.1 = ((bf16[8,16,4096]{2,1,0:T(8,128)(2,1)}), bf16[8,16,4096]{2,1,0:T(8,128)(2,1)S(1)}, u32[]{:S(2)}, u32[]{:S(2)}) async-start(bf16[8,16,4096]{2,1,0:T(8,128)(2,1)} %bitcast.5), calls=%async_computation.1 | async-start | bytes 2097152 | tf_op jit(solution)/shard_map/all_to_all | solution.py:270
  37.1 0.0 copy-done.7
  37.1 0.7 copy.13.routes
  37.7 2.9 %number_slots.1.slots = s32[16,8]{1,0:T(8,128)} custom-call(s32[16,8]{1,0:T(8,128)} %copy.13.routes), custom_call_target="tpu_custom_call" | custom-call | tf_op jit(solution)/shard_map/number_slots/pallas_call | solution.py:244
  40.6 10.0 %all-to-all-done.1.shares = bf16[8,16,4096]{2,1,0:T(8,128)(2,1)S(1)} async-done(((bf16[8,16,4096]{2,1,0:T(8,128)(2,1)}), bf16[8,16,4096]{2,1,0:T(8,128)(2,1)S(1)}, u32[]{:S(2)}, u32[]{:S(2)}) %all-to-all-start.1) | async-done | bytes 1048608 | tf_op jit(solution)/shard_map/all_to_all | solution.py:270
  50.6 0.0 copy-done.2
  50.6 0.0 copy-done.5
  50.6 0.0 copy-start.3
  50.6 0.7 copy-done.3
  51.3 2.3 %norm_dispatch.1 = (bf16[16,4096]{1,0:T(8,128)(2,1)}, bf16[256,32,128]{2,1,0:T(8,128)(2,1)S(1)}) custom-call(s32[16,8]{1,0:T(8,128)S(1)} %copy-done.3, bf16[8,16,4096]{2,1,0:T(8,128)(2,1)S(1)} %all-to-all-done.1.shares, bf16[16,4096]{1,0:T(8,128)(2,1)S(1)} %copy-done.2, f32[1,4096]{1,0:T(1,128)S(1)} %bitcast.20), custom_call_target="tpu_custom_call" | custom-call | tf_op jit(solution)/shard_map/norm_dispatch/pallas_call | solution.py:273
  53.6 41.9 %all_to_all.20 = bf16[128,64,128]{2,1,0:T(8,128)(2,1)S(1)} all-to-all(bf16[128,64,128]{2,1,0:T(8,128)(2,1)S(1)} %bitcast.18), channel_id=1, replica_groups=mesh['x'=4,'yl'=2,'yh'=2,'z'=4,'c'=2] {'x','yl','yh','z','c'}, dimensions={0} | all-to-all | bytes 4194304 | tf_op jit(solution)/shard_map/all_to_all | solution.py:286
  95.5 16.3 %expert_rows.1 = bf16[8192,128]{1,0:T(8,128)(2,1)S(1)} custom-call(bf16[8192,128]{1,0:T(8,128)(2,1)S(1)} %bitcast.17, bf16[1,4096,768]{2,1,0:T(8,128)(2,1)} %w_gate.1, bf16[1,4096,768]{2,1,0:T(8,128)(2,1)} %w_up.1, bf16[1,768,4096]{2,1,0:T(8,128)(2,1)} %w_down.1), custom_call_target="tpu_custom_call" | custom-call | tf_op jit(solution)/shard_map/expert_rows/pallas_call | solution.py:289
  111.8 0.0 copy-start
  111.8 1.3 copy-done
  113.1 0.0 copy-start.8
  113.1 0.0 copy-start.4
  113.1 4.9 %all-to-all-start.3 = ((bf16[128,64,128]{2,1,0:T(8,128)(2,1)}), bf16[128,64,128]{2,1,0:T(8,128)(2,1)S(1)}, u32[]{:S(2)}, u32[]{:S(2)}) async-start(bf16[128,64,128]{2,1,0:T(8,128)(2,1)} %bitcast.16), calls=%async_computation.3 | async-start | bytes 4194304 | tf_op jit(solution)/shard_map/all_to_all | solution.py:305
  118.1 0.0 copy-done.8
  118.1 0.1 copy.16.weights
  118.1 29.7 %all-to-all-done.3 = bf16[128,64,128]{2,1,0:T(8,128)(2,1)S(1)} async-done(((bf16[128,64,128]{2,1,0:T(8,128)(2,1)}), bf16[128,64,128]{2,1,0:T(8,128)(2,1)S(1)}, u32[]{:S(2)}, u32[]{:S(2)}) %all-to-all-start.3) | async-done | bytes 2097184 | tf_op jit(solution)/shard_map/all_to_all | solution.py:305
  147.9 0.0 copy-done.4
  147.9 2.0 %mix.1 = f32[16,4096]{1,0:T(8,128)} custom-call(s32[16,8]{1,0:T(8,128)S(1)} %copy-done.4, f32[16,8]{1,0:T(8,128)S(1)} %copy.16.weights, bf16[256,32,128]{2,1,0:T(8,128)(2,1)S(1)} %bitcast.15), custom_call_target="tpu_custom_call" | custom-call | tf_op jit(solution)/shard_map/mix/pallas_call | solution.py:308
  (2 shorter events, 0.0 us)
Async XLA Ops:
  0.6 24.7 %copy-start.1 = (bf16[256,4096]{1,0:T(8,128)(2,1)S(1)}, bf16[256,4096]{1,0:T(8,128)(2,1)}, u32[]{:S(2)}) copy-start(bf16[256,4096]{1,0:T(8,128)(2,1)} %own_proj.1) | copy-start | bytes 6291460
  0.6 8.6 %copy-start.6 = (bf16[256,256]{1,0:T(8,128)(2,1)S(1)}, bf16[256,256]{1,0:T(8,128)(2,1)}, u32[]{:S(2)}) copy-start(bf16[256,256]{1,0:T(8,128)(2,1)} %param.11) | copy-start | bytes 393220
  0.7 24.7 %collective-permute-start.1 = (bf16[256,4096]{1,0:T(8,128)(2,1)}, bf16[256,4096]{1,0:T(8,128)(2,1)}, u32[]{:S(2)}, u32[]{:S(2)}) collective-permute-start(bf16[256,4096]{1,0:T(8,128)(2,1)} %own_proj.1), channel_id=1, source_target_pairs={{0,1},{1,0},{2,3},{3,2},{4,5},{5,4},{6,7},{7,6},{8,9},{9,8},{10,11... | collective-permute-start | bytes 6291464 | tf_op jit(solution)/shard_map/ppermute | solution.py:211
  4.1 21.2 %all-to-all-start = ((bf16[8,256,256]{2,1,0:T(8,128)(2,1)}), bf16[8,256,256]{2,1,0:T(8,128)(2,1)S(1)}, u32[]{:S(2)}, u32[]{:S(2)}) async-start(bf16[8,256,256]{2,1,0:T(8,128)(2,1)} %broadcast_in_dim.2), calls=%async_computation | async-start | bytes 2097152 | tf_op jit(solution)/shard_map/all_to_all | solution.py:216
  9.2 1.4 collective-permute-start
  29.5 7.6 %copy-start.7 = (s32[16,8]{0,1:T(8,128)S(1)}, s32[16,8]{0,1:T(8,128)}, u32[]{:S(2)}) copy-start(s32[16,8]{0,1:T(8,128)} %param.17) | copy-start | bytes 1540
  29.5 21.1 %copy-start.2 = (bf16[16,4096]{1,0:T(8,128)(2,1)S(1)}, bf16[16,4096]{1,0:T(8,128)(2,1)}, u32[]{:S(2)}) copy-start(bf16[16,4096]{1,0:T(8,128)(2,1)} %residual.1) | copy-start | bytes 393220
  29.5 21.1 %copy-start.5 = (f32[4096]{0:T(1024)S(1)}, f32[4096]{0:T(1024)}, u32[]{:S(2)}) copy-start(f32[4096]{0:T(1024)} %param.16) | copy-start | bytes 49156
  29.5 21.1 %all-to-all-start.1 = ((bf16[8,16,4096]{2,1,0:T(8,128)(2,1)}), bf16[8,16,4096]{2,1,0:T(8,128)(2,1)S(1)}, u32[]{:S(2)}, u32[]{:S(2)}) async-start(bf16[8,16,4096]{2,1,0:T(8,128)(2,1)} %bitcast.5), calls=%async_computation.1 | async-start | bytes 2097152 | tf_op jit(solution)/shard_map/all_to_all | solution.py:270
  50.6 0.7 copy-start.3
  111.8 1.3 copy-start
  113.1 4.9 %copy-start.8 = (f32[16,8]{0,1:T(8,128)S(1)}, f32[16,8]{0,1:T(8,128)}, u32[]{:S(2)}) copy-start(f32[16,8]{0,1:T(8,128)} %param.18) | copy-start | bytes 1540
  113.1 34.7 %copy-start.4 = (s32[16,8]{1,0:T(8,128)S(1)}, s32[16,8]{1,0:T(8,128)}, u32[]{:S(2)}) copy-start(s32[16,8]{1,0:T(8,128)} %number_slots.1.slots) | copy-start | bytes 1540
  113.1 34.7 %all-to-all-start.3 = ((bf16[128,64,128]{2,1,0:T(8,128)(2,1)}), bf16[128,64,128]{2,1,0:T(8,128)(2,1)S(1)}, u32[]{:S(2)}, u32[]{:S(2)}) async-start(bf16[128,64,128]{2,1,0:T(8,128)(2,1)} %bitcast.16), calls=%async_computation.3 | async-start | bytes 4194304 | tf_op jit(solution)/shard_map/all_to_all | solution.py:305

commit v2 on v1

v2 whole, which is shorter than its diff:
```python
import math

import jax
import jax.numpy as jnp
from jax import lax
from jax.experimental import pallas as pl
from jax.experimental.pallas import tpu as pltpu
from jax.sharding import Mesh
from jax.sharding import PartitionSpec as P

D = 4096
HEAD_WIDTH = 128
TOP = 8
TOKENS = 16
EXPERTS = 128
CAP = 2
SLOTS = EXPERTS * CAP
BLOCK = 256
FF = 768
PIECES = D // 128
CTX = ("x", "yl")
CHIPS = ("yh", "z")
ALL = ("x", "yl", "yh", "z", "c")
INV_ROOT = 1.0 / math.sqrt(HEAD_WIDTH)
MIB = 1 << 20

VMEM = pl.BlockSpec(memory_space=pltpu.VMEM)
SMEM = pl.BlockSpec(memory_space=pltpu.SMEM)
HBM = pl.BlockSpec(memory_space=pltpu.HBM)


def attention_kernel(place, own_queries, twin_queries, *refs):
    arrived, (own_proj, twin_proj, out, w_buf, sems, raw, tops, sums, acc, blocks) = refs[:8], refs[8:]
    copies = [
        pltpu.make_async_copy(own_proj, w_buf.at[pl.ds(0, 256)], sems.at[0]),
        pltpu.make_async_copy(twin_proj, w_buf.at[pl.ds(256, 256)], sems.at[1]),
    ]
    for copy in copies:
        copy.start()
    own_block = place[0]
    core = place[1]
    for index, block in enumerate(arrived):
        blocks[place[2 + index]] = block[...]
    stacked = jnp.concatenate(
        [
            own_queries[:, 0:128],
            own_queries[:, 128:256],
            twin_queries[:, 0:128],
            twin_queries[:, 128:256],
        ],
        axis=0,
    )

    def products(block):
        return lax.dot_general(
            stacked,
            blocks[block, :, 0:128],
            (((1,), (1,)), ((), ())),
            preferred_element_type=jnp.float32,
        )

    def columns_of(block):
        return pl.ds(pl.multiple_of(block * BLOCK, BLOCK), BLOCK)

    row = lax.broadcasted_iota(jnp.int32, (512, BLOCK), 0) % 128
    position = (row // TOKENS) * (2 * TOKENS) + core * TOKENS + row % TOKENS
    visible = lax.broadcasted_iota(jnp.int32, (512, BLOCK), 1) <= position
    latest = jnp.where(visible, products(own_block), -1e30)
    raw[:, columns_of(own_block)] = latest
    tops[...] = jnp.maximum(latest[:, 0:128], latest[:, 128:256])

    @pl.loop(0, own_block)
    def score(block):
        earlier = products(block)
        raw[:, columns_of(block)] = earlier
        tops[...] = jnp.maximum(
            tops[...], jnp.maximum(earlier[:, 0:128], earlier[:, 128:256])
        )

    tops[...] = jnp.broadcast_to(jnp.max(tops[...], axis=1, keepdims=True), (512, 128))
    sums[...] = jnp.zeros((512, 128), jnp.float32)
    acc[...] = jnp.zeros((512, 128), jnp.float32)

    @pl.loop(0, own_block + 1)
    def weigh(block):
        top = tops[...]
        scores = raw[:, columns_of(block)]
        left = jnp.exp((scores[:, 0:128] - top) * INV_ROOT)
        right = jnp.exp((scores[:, 128:256] - top) * INV_ROOT)
        sums[...] += left + right
        probs = jnp.concatenate([left.astype(jnp.bfloat16), right.astype(jnp.bfloat16)], axis=1)
        acc[...] += jnp.dot(
            probs, blocks[block, :, 128:256], preferred_element_type=jnp.float32
        )

    total = jnp.sum(sums[...], axis=1, keepdims=True)
    attended = (acc[...] / total).astype(jnp.bfloat16)
    wide = jnp.concatenate([attended[h * 128 : (h + 1) * 128] for h in range(4)], axis=1)
    for copy in copies:
        copy.wait()

    for piece in range(D // 512):
        columns = slice(piece * 512, (piece + 1) * 512)
        out[:, columns] = jnp.dot(
            wide, w_buf[:, columns], preferred_element_type=jnp.float32
        ).astype(jnp.bfloat16)


def slots_kernel(routes, slots, counts):
    @pl.loop(0, EXPERTS)
    def clear(expert):
        counts[expert] = 0

    @pl.loop(0, TOKENS)
    def number(token):
        for choice in range(TOP):
            expert = routes[token, choice]
            rank = counts[expert]
            counts[expert] = rank + 1
            slots[token, choice] = expert * CAP + rank


def norm_kernel(listed, shares, residual, gain, hidden, outgoing, rows, slots, sem):
    listing = pltpu.make_async_copy(listed, slots, sem)
    listing.start()
    total = residual[...].astype(jnp.float32)
    for share in range(8):
        total = total + shares[share].astype(jnp.float32)
    state = total.astype(jnp.bfloat16)
    hidden[...] = state
    wide = state.astype(jnp.float32)
    scale = lax.rsqrt(jnp.mean(wide * wide, axis=1, keepdims=True) + 1e-6)
    normed = wide * scale * gain[...]
    for piece in range(PIECES):
        rows[pl.ds(piece, TOKENS, stride=PIECES), :] = normed[:, piece * 128 : (piece + 1) * 128]

    @pl.loop(0, SLOTS // 8)
    def clear(group):
        outgoing[pl.ds(group * 8, 8)] = jnp.zeros((8, PIECES, 128), jnp.bfloat16)

    listing.wait()

    @pl.loop(0, TOKENS)
    def place(token):
        row = rows[pl.ds(pl.multiple_of(token * PIECES, PIECES), PIECES), :].astype(jnp.bfloat16)
        for choice in range(TOP):
            outgoing[slots[token, choice]] = row


def expert_kernel(
    incoming,
    w_gate,
    w_up,
    w_down,
    out,
    gate_buf,
    up_buf,
    down_buf,
    fetch_sems,
    gate,
    upward,
    wide,
    rows,
    stage,
    sems,
):
    def pair(part):
        span = pl.ds(part * 1024, 1024)
        return [
            pltpu.make_async_copy(
                w_gate.at[0, span], gate_buf.at[span], fetch_sems.at[2 * part]
            ),
            pltpu.make_async_copy(
                w_up.at[0, span], up_buf.at[span], fetch_sems.at[2 * part + 1]
            ),
        ]

    def down(part):
        return pltpu.make_async_copy(
            w_down.at[0, :, pl.ds(part * 1024, 1024)], down_buf.at[part], fetch_sems.at[8 + part]
        )

    pairs = [pair(part) for part in range(4)]
    downs = [down(part) for part in range(4)]
    then = [pairs[2], pairs[3], downs[0:2], downs[2:4]]
    for copy in pairs[0] + pairs[1]:
        copy.start()

    @pl.loop(0, SLOTS // 32)
    def widen(group):
        wide[pl.ds(group * 32 * PIECES, 32 * PIECES), :] = incoming[
            pl.ds(group * 32 * PIECES, 32 * PIECES), :
        ].astype(jnp.float32)

    for part in range(4):
        for piece in range(part * 8, part * 8 + 8):
            rows[:, piece * 128 : (piece + 1) * 128] = wide[
                pl.ds(piece, SLOTS, stride=PIECES), :
            ].astype(jnp.bfloat16)
        span = slice(part * 1024, (part + 1) * 1024)
        for copy in pairs[part]:
            copy.wait()
        for copy in then[part]:
            copy.start()
        for total, weights in ((gate, gate_buf), (upward, up_buf)):
            product = jnp.dot(rows[:, span], weights[span, :], preferred_element_type=jnp.float32)
            if part:
                total[...] += product
            else:
                total[...] = product
    active = (gate[...] / (1.0 + jnp.exp(-gate[...])) * upward[...]).astype(jnp.bfloat16)
    for part in range(8):
        if part % 2 == 0:
            downs[part // 2].wait()
        half = part % 2
        produced = jnp.dot(
            active,
            down_buf[part // 2, :, half * 512 : (half + 1) * 512],
            preferred_element_type=jnp.float32,
        )
        for lane in range(4):
            piece = part * 4 + lane
            for tile in range(SLOTS // 8):
                start = tile * 8 * PIECES + piece * 8
                wide[start : start + 8, :] = produced[
                    tile * 8 : (tile + 1) * 8, lane * 128 : (lane + 1) * 128
                ]
    copies = []
    for quarter in range(4):

        @pl.loop(quarter * 8, quarter * 8 + 8)
        def narrow(tile):
            for row in range(8):
                start = pl.multiple_of((tile * 8 + row) * PIECES, PIECES)
                stage[pl.ds(start, PIECES), :] = wide[
                    pl.ds(tile * 8 * PIECES + row, PIECES, stride=8), :
                ].astype(jnp.bfloat16)

        span = pl.ds(quarter * 64 * PIECES, 64 * PIECES)
        copy = pltpu.make_async_copy(stage.at[span], out.at[span], sems.at[quarter])
        copy.start()
        copies.append(copy)
    for copy in copies:
        copy.wait()


def mix_kernel(slots, weights, returned, out, rows):
    @pl.loop(0, TOKENS)
    def gather(token):
        total = jnp.zeros((PIECES, 128), jnp.float32)
        for choice in range(TOP):
            total = total + weights[token, choice] * returned[slots[token, choice]].astype(
                jnp.float32
            )
        rows[pl.ds(pl.multiple_of(token * PIECES, PIECES), PIECES), :] = total

    for piece in range(PIECES):
        out[:, piece * 128 : (piece + 1) * 128] = rows[pl.ds(piece, TOKENS, stride=PIECES), :]


def swap_cores(array):
    return lax.ppermute(array, "c", [(0, 1), (1, 0)])


def gather_blocks(block):
    fetched, handed = [], []
    for step in range(4):
        pairs = []
        for x in range(4):
            for y in range(2):
                for core in range(2):
                    target_x = (x + step) % 4
                    target_y = y if core == y else 1 - y
                    pairs.append(((x * 2 + y) * 2 + core, (target_x * 2 + target_y) * 2 + y))
        fetched.append(lax.ppermute(block, ("x", "yl", "c"), pairs))
        handed.append(swap_cores(fetched[-1]))
    x, core = lax.axis_index("x"), lax.axis_index("c")
    rings = [lax.rem(x - step + 4, 4) * 2 for step in range(4)]
    origins = [ring + core for ring in rings] + [ring + 1 - core for ring in rings]
    return fetched + handed, origins


def on_device(
    queries,
    keys,
    values,
    out_proj,
    residual,
    norm_gain,
    routes,
    route_weights,
    w_gate,
    w_up,
    w_down,
):
    ctx_index = lax.axis_index(CTX)
    core = lax.axis_index("c")
    shared_head = lax.axis_index(CHIPS) // 2
    own_keys = lax.dynamic_slice_in_dim(keys, shared_head * HEAD_WIDTH, HEAD_WIDTH, 1)
    own_values = lax.dynamic_slice_in_dim(values, shared_head * HEAD_WIDTH, HEAD_WIDTH, 1)
    blocks, origins = gather_blocks(jnp.concatenate([own_keys, own_values], axis=1))
    split = queries.reshape(8, 2, TOKENS, 256)
    own_queries = lax.dynamic_index_in_dim(split, core, 1, False).reshape(128, 256)
    sent_queries = lax.dynamic_index_in_dim(split, 1 - core, 1, False).reshape(128, 256)
    twin_queries = swap_cores(sent_queries)
    twin_proj = swap_cores(out_proj)

    slots = pl.pallas_call(
        slots_kernel,
        out_shape=jax.ShapeDtypeStruct((TOKENS, TOP), jnp.int32),
        in_specs=[SMEM],
        out_specs=SMEM,
        scratch_shapes=[pltpu.SMEM((EXPERTS,), jnp.int32)],
        name="number_slots",
    )(routes)

    place = jnp.stack([ctx_index, core] + origins).astype(jnp.int32)
    partial = pl.pallas_call(
        attention_kernel,
        out_shape=jax.ShapeDtypeStruct((128, D), jnp.bfloat16),
        in_specs=[SMEM] + [VMEM] * 10 + [HBM, HBM],
        out_specs=VMEM,
        scratch_shapes=[
            pltpu.VMEM((512, D), jnp.bfloat16),
            pltpu.SemaphoreType.DMA((2,)),
            pltpu.VMEM((512, 8 * BLOCK), jnp.float32),
            pltpu.VMEM((512, 128), jnp.float32),
            pltpu.VMEM((512, 128), jnp.float32),
            pltpu.VMEM((512, 128), jnp.float32),
            pltpu.VMEM((8, BLOCK, 256), jnp.bfloat16),
        ],
        compiler_params=pltpu.CompilerParams(vmem_limit_bytes=24 * MIB),
        name="attend_project",
    )(place, own_queries, twin_queries, *blocks, out_proj, twin_proj)

    shares = lax.all_to_all(
        partial.reshape(8, TOKENS, D), CHIPS, split_axis=0, concat_axis=0, tiled=True
    )
    hidden_state, outgoing = pl.pallas_call(
        norm_kernel,
        out_shape=(
            jax.ShapeDtypeStruct((TOKENS, D), jnp.bfloat16),
            jax.ShapeDtypeStruct((SLOTS, PIECES, 128), jnp.bfloat16),
        ),
        in_specs=[HBM, VMEM, VMEM, VMEM],
        out_specs=(VMEM, VMEM),
        scratch_shapes=[
            pltpu.VMEM((TOKENS * PIECES, 128), jnp.float32),
            pltpu.SMEM((TOKENS, TOP), jnp.int32),
            pltpu.SemaphoreType.DMA,
        ],
        compiler_params=pltpu.CompilerParams(vmem_limit_bytes=16 * MIB),
        name="norm_dispatch",
    )(slots, shares, residual, norm_gain.reshape(1, D))

    incoming = lax.all_to_all(
        outgoing.reshape(EXPERTS, CAP * PIECES, 128), ALL, split_axis=0, concat_axis=0, tiled=True
    )
    produced = pl.pallas_call(
        expert_kernel,
        out_shape=pltpu.HBM((SLOTS * PIECES, 128), jnp.bfloat16),
        in_specs=[VMEM, HBM, HBM, HBM],
        out_specs=HBM,
        scratch_shapes=[
            pltpu.VMEM((D, FF), jnp.bfloat16),
            pltpu.VMEM((D, FF), jnp.bfloat16),
            pltpu.VMEM((4, FF, 1024), jnp.bfloat16),
            pltpu.SemaphoreType.DMA((12,)),
            pltpu.VMEM((SLOTS, FF), jnp.float32),
            pltpu.VMEM((SLOTS, FF), jnp.float32),
            pltpu.VMEM((SLOTS * PIECES, 128), jnp.float32),
            pltpu.VMEM((SLOTS, D), jnp.bfloat16),
            pltpu.VMEM((SLOTS * PIECES, 128), jnp.bfloat16),
            pltpu.SemaphoreType.DMA((4,)),
        ],
        compiler_params=pltpu.CompilerParams(vmem_limit_bytes=56 * MIB),
        name="expert_rows",
    )(incoming.reshape(SLOTS * PIECES, 128), w_gate, w_up, w_down)
    returned = lax.all_to_all(
        produced.reshape(EXPERTS, CAP * PIECES, 128), ALL, split_axis=0, concat_axis=0, tiled=True
    )
    expert_mix = pl.pallas_call(
        mix_kernel,
        out_shape=jax.ShapeDtypeStruct((TOKENS, D), jnp.float32),
        in_specs=[SMEM, SMEM, VMEM],
        out_specs=VMEM,
        scratch_shapes=[pltpu.VMEM((TOKENS * PIECES, 128), jnp.float32)],
        compiler_params=pltpu.CompilerParams(vmem_limit_bytes=16 * MIB),
        name="mix",
    )(slots, route_weights, returned.reshape(SLOTS, PIECES, 128))
    return (hidden_state, expert_mix)


def solution(mesh):
    fine = Mesh(mesh.devices.reshape(4, 2, 2, 4, 2), ALL)
    exp = ("yh", "z", "c")
    placed = (
        P(CTX, exp),
        P(CTX, None),
        P(CTX, None),
        P(exp, None),
        P(ALL, None),
        P(),
        P(ALL, None),
        P(ALL, None),
        P(ALL, None, None),
        P(ALL, None, None),
        P(ALL, None, None),
    )
    return jax.shard_map(
        on_device,
        mesh=fine,
        in_specs=placed,
        out_specs=(P(ALL, None), P(ALL, None)),
        check_vma=False,
    )
```

time: 150 us -> 141 us (0.940)
  waiting for transfers between devices: 55.2 us -> 46.5 us
  starting transfers between devices: 19.6 us -> 23.6 us
  Pallas kernels: 27.6 us -> 24.1 us
  blocking collectives: 41.9 us -> 40.2 us
    all_to_all x1 -> x0, waiting for transfers between devices: 14.7 us -> none  [gather_blocks(): return lax.all_to_all(spread, CTX, split_axis=0, concat_axis=0, tiled=True)]
    ppermute x0 -> x4, starting transfers between devices: none -> 9.52 us  [gather_blocks(): fetched.append(lax.ppermute(block, ('x', 'yl', 'c'), pairs))]
    all_to_all x1 -> x0, starting transfers between devices: 5.12 us -> none  [gather_blocks(): return lax.all_to_all(spread, CTX, split_axis=0, concat_axis=0, tiled=True)]
    ppermute x0 -> x4, waiting for transfers between devices: none -> 4.48 us  [gather_blocks(): fetched.append(lax.ppermute(block, ('x', 'yl', 'c'), pairs))]
    pallas_call x1, Pallas kernels: 16.3 us -> 14.1 us  [on_device(): pl.pallas_call(expert_kernel, out_shape=pltpu.HBM((SLOTS * PIECES, 128),...]
    all_to_all x1, blocking collectives: 41.9 us -> 40.2 us  [on_device(): lax.all_to_all(outgoing.reshape(EXPERTS, CAP * PIECES, 128), ALL, split_a...]
    unnamed x20 -> x16, local copies, waits for them, and re-layouts: 2.81 us -> 3.06 us
  transfers between devices with their start and end apart: 5 -> 12, of which waited for: 4 -> 6; matrix products, arithmetic and copies ran while one was open for 2% -> 2% of each run, Pallas kernels for 2% -> 2%
where the time goes in v2:
time: 141 us; the launch traced here: 140 us
  waiting for transfers between devices  46.5 us (33%)
  blocking collectives  40.2 us (29%)
  Pallas kernels  24.1 us (17%)
  starting transfers between devices  23.6 us (17%)
  local copies, waits for them, and re-layouts  4.92 us (3%)
    all_to_all x1, blocking collectives, on_device(): lax.all_to_all(outgoing.reshape(EXPERTS, CAP * PIECES, 128), ALL, split_a...  40.2 us
    all_to_all x1, waiting for transfers between devices, on_device(): lax.all_to_all(produced.reshape(EXPERTS, CAP * PIECES, 128), ALL, split_a...  29.6 us
    pallas_call x1, Pallas kernels, on_device(): pl.pallas_call(expert_kernel, out_shape=pltpu.HBM((SLOTS * PIECES, 128),...  14.1 us
    all_to_all x1, waiting for transfers between devices, on_device(): lax.all_to_all(partial.reshape(8, TOKENS, D), CHIPS, split_axis=0, concat...  11.2 us
    ppermute x4, starting transfers between devices, gather_blocks(): fetched.append(lax.ppermute(block, ('x', 'yl', 'c'), pairs))  9.52 us
    all_to_all x1, starting transfers between devices, on_device(): lax.all_to_all(partial.reshape(8, TOKENS, D), CHIPS, split_axis=0, concat...  7.51 us
    all_to_all x1, starting transfers between devices, on_device(): lax.all_to_all(produced.reshape(EXPERTS, CAP * PIECES, 128), ALL, split_a...  4.93 us
    ppermute x4, waiting for transfers between devices, gather_blocks(): fetched.append(lax.ppermute(block, ('x', 'yl', 'c'), pairs))  4.48 us
  transfers between devices with their start and end apart: 12, of which 6 were waited for; matrix products, arithmetic and copies ran while one was open for 2% of the time, Pallas kernels for 2%

profile of v2, /device:TPU:1, one launch (start us, length us, event | category | flops | bytes accessed | tf_op | source)
XLA Modules:
  0.0 140.1 jit_solution(5256678117528959144)
XLA Ops:
  0.6 1.5 %collective-permute-start.9 = (bf16[256,4096]{1,0:T(8,128)(2,1)}, bf16[256,4096]{1,0:T(8,128)(2,1)S(1)}, u32[]{:S(2)}, u32[]{:S(2)}) collective-permute-start(bf16[256,4096]{1,0:T(8,128)(2,1)} %refs_8_.1), channel_id=1, source_target_pairs={{0,1},{1,0},{2,3},{3,2},{4,5},{5,4},{6,7},{7,6},{8,9},{9,8},{10,11... | collective-permute-start | bytes 6291464 | tf_op jit(solution)/shard_map/ppermute | solution.py:262
  2.1 0.9 constant_dynamic-slice_fusion.2
  3.0 0.1 collective-permute-start
  3.1 0.9 constant_dynamic-slice_fusion
  4.0 3.6 %collective-permute-start.1 = (bf16[256,256]{1,0:T(8,128)(2,1)S(1)}, bf16[256,256]{1,0:T(8,128)(2,1)S(1)}, u32[]{:S(2)}, u32[]{:S(2)}) collective-permute-start(bf16[256,256]{1,0:T(8,128)(2,1)S(1)} %pad_maximum_fusion), channel_id=1, source_target_pairs={{0,0},{1,16},{16,1},{17,17},{32,32},{33,48},{48,33},{49,49},{64,64... | collective-permute-start | bytes 393224 | tf_op jit(solution)/shard_map/ppermute | solution.py:275
  7.7 1.1 collective-permute-start.2
  8.8 3.8 %collective-permute-start.3 = (bf16[256,256]{1,0:T(8,128)(2,1)S(1)}, bf16[256,256]{1,0:T(8,128)(2,1)S(1)}, u32[]{:S(2)}, u32[]{:S(2)}) collective-permute-start(bf16[256,256]{1,0:T(8,128)(2,1)S(1)} %pad_maximum_fusion), channel_id=1, source_target_pairs={{0,64},{1,80},{16,65},{17,81},{32,96},{33,112},{48,97},{49,113},{6... | collective-permute-start | bytes 393224 | tf_op jit(solution)/shard_map/ppermute | solution.py:275
  12.6 0.0 collective-permute-done.twin_queries
  12.6 1.0 collective-permute-start.4
  13.6 0.0 collective-permute-done.1.refs_0_
  13.6 0.0 collective-permute-start.5
  13.6 1.1 collective-permute-done.2.refs_1_
  14.7 0.0 collective-permute-start.6
  14.7 2.1 %collective-permute-done.3.refs_2_ = bf16[256,256]{1,0:T(8,128)(2,1)S(1)} collective-permute-done((bf16[256,256]{1,0:T(8,128)(2,1)S(1)}, bf16[256,256]{1,0:T(8,128)(2,1)S(1)}, u32[]{:S(2)}, u32[]{:S(2)}) %collective-permute-start.3) | collective-permute-done | bytes 131104 | tf_op jit(solution)/shard_map/ppermute | solution.py:275
  16.8 0.0 collective-permute-start.7
  16.8 1.2 collective-permute-done.4.refs_3_
  18.1 0.0 collective-permute-start.8
  18.1 0.1 stack.43.place
  18.1 0.0 collective-permute-done.5.refs_4_
  18.2 0.0 collective-permute-done.6.refs_5_
  18.2 0.0 collective-permute-done.7.refs_6_
  18.2 1.2 collective-permute-done.8.refs_7_
  19.4 0.0 collective-permute-done.9.refs_9_
  19.4 0.0 copy-start
  19.4 1.6 %copy-done = bf16[256,4096]{1,0:T(8,128)(2,1)S(1)} copy-done((bf16[256,4096]{1,0:T(8,128)(2,1)S(1)}, bf16[256,4096]{1,0:T(8,128)(2,1)}, u32[]{:S(2)}) %copy-start) | copy-done | bytes 2097176
  21.0 3.4 %attend_project.1 = bf16[128,4096]{1,0:T(8,128)(2,1)} custom-call(s32[10]{0:T(128)S(1)} %stack.43.place, bf16[128,256]{1,0:T(8,128)(2,1)S(1)} %bitcast.25, bf16[128,256]{1,0:T(8,128)(2,1)S(1)} %collective-permute-done.twin_queries, bf16[256,256]{1,0:T(8,128)(2,1)S(1)} %collective-permute-done.1.refs_0_, bf16[256,256]{1,0:T(8,128)(2,1)S(1)} %collective-permute-done.2.refs_1_, ...), custom_call_target="tpu_custom_call" | custom-call | tf_op jit(solution)/shard_map/attend_project/pallas_call | solution.py:318
  24.4 0.0 copy-start.5
  24.4 0.0 copy-start.1
  24.4 0.0 copy-start.4
  24.5 7.5 %all-to-all-start = ((bf16[8,16,4096]{2,1,0:T(8,128)(2,1)}), bf16[8,16,4096]{2,1,0:T(8,128)(2,1)S(1)}, u32[]{:S(2)}, u32[]{:S(2)}) async-start(bf16[8,16,4096]{2,1,0:T(8,128)(2,1)} %bitcast.13), calls=%async_computation | async-start | bytes 2097152 | tf_op jit(solution)/shard_map/all_to_all | solution.py:336
  32.0 0.0 copy-done.5
  32.0 0.7 copy.13.routes
  32.6 2.9 %number_slots.1.listed.slots = s32[16,8]{1,0:T(8,128)} custom-call(s32[16,8]{1,0:T(8,128)} %copy.13.routes), custom_call_target="tpu_custom_call" | custom-call | tf_op jit(solution)/shard_map/number_slots/pallas_call | solution.py:308
  35.6 11.2 %all-to-all-done.shares = bf16[8,16,4096]{2,1,0:T(8,128)(2,1)S(1)} async-done(((bf16[8,16,4096]{2,1,0:T(8,128)(2,1)}), bf16[8,16,4096]{2,1,0:T(8,128)(2,1)S(1)}, u32[]{:S(2)}, u32[]{:S(2)}) %all-to-all-start) | async-done | bytes 1048608 | tf_op jit(solution)/shard_map/all_to_all | solution.py:336
  46.7 0.0 copy-done.1
  46.7 0.0 copy-done.4
  46.7 0.0 copy-start.2
  46.7 0.7 copy-done.2
  47.4 1.6 %norm_dispatch.1 = (bf16[16,4096]{1,0:T(8,128)(2,1)}, bf16[256,32,128]{2,1,0:T(8,128)(2,1)S(1)}) custom-call(s32[16,8]{1,0:T(8,128)S(1)} %copy-done.2, bf16[8,16,4096]{2,1,0:T(8,128)(2,1)S(1)} %all-to-all-done.shares, bf16[16,4096]{1,0:T(8,128)(2,1)S(1)} %copy-done.1, f32[1,4096]{1,0:T(1,128)S(1)} %bitcast.26), custom_call_target="tpu_custom_call" | custom-call | tf_op jit(solution)/shard_map/norm_dispatch/pallas_call | solution.py:339
  49.1 40.2 %all_to_all.15 = bf16[128,64,128]{2,1,0:T(8,128)(2,1)} all-to-all(bf16[128,64,128]{2,1,0:T(8,128)(2,1)S(1)} %bitcast.24), channel_id=1, replica_groups=mesh['x'=4,'yl'=2,'yh'=2,'z'=4,'c'=2] {'x','yl','yh','z','c'}, dimensions={0} | all-to-all | bytes 4194304 | tf_op jit(solution)/shard_map/all_to_all | solution.py:356
  89.2 14.1 %expert_rows.1 = bf16[8192,128]{1,0:T(8,128)(2,1)} custom-call(bf16[8192,128]{1,0:T(8,128)(2,1)} %bitcast.28, bf16[1,4096,768]{2,1,0:T(8,128)(2,1)} %w_gate.1, bf16[1,4096,768]{2,1,0:T(8,128)(2,1)} %w_up.1, bf16[1,768,4096]{2,1,0:T(8,128)(2,1)} %w_down.1), custom_call_target="tpu_custom_call" | custom-call | tf_op jit(solution)/shard_map/expert_rows/pallas_call | solution.py:359
  103.4 0.0 copy-start.6
  103.4 0.0 copy-start.3
  103.4 4.9 %all-to-all-start.2 = ((bf16[128,64,128]{2,1,0:T(8,128)(2,1)}), bf16[128,64,128]{2,1,0:T(8,128)(2,1)S(1)}, u32[]{:S(2)}, u32[]{:S(2)}) async-start(bf16[128,64,128]{2,1,0:T(8,128)(2,1)} %bitcast.27), calls=%async_computation.2 | async-start | bytes 4194304 | tf_op jit(solution)/shard_map/all_to_all | solution.py:379
  108.3 0.0 copy-done.6
  108.3 0.1 copy.16.weights
  108.4 29.6 %all-to-all-done.2 = bf16[128,64,128]{2,1,0:T(8,128)(2,1)S(1)} async-done(((bf16[128,64,128]{2,1,0:T(8,128)(2,1)}), bf16[128,64,128]{2,1,0:T(8,128)(2,1)S(1)}, u32[]{:S(2)}, u32[]{:S(2)}) %all-to-all-start.2) | async-done | bytes 2097184 | tf_op jit(solution)/shard_map/all_to_all | solution.py:379
  138.1 0.0 copy-done.3
  138.1 2.0 %mix.1 = f32[16,4096]{1,0:T(8,128)} custom-call(s32[16,8]{1,0:T(8,128)S(1)} %copy-done.3, f32[16,8]{1,0:T(8,128)S(1)} %copy.16.weights, bf16[256,32,128]{2,1,0:T(8,128)(2,1)S(1)} %bitcast.23), custom_call_target="tpu_custom_call" | custom-call | tf_op jit(solution)/shard_map/mix/pallas_call | solution.py:382
  (1 shorter events, 0.0 us)
Async XLA Ops:
  0.6 18.8 %collective-permute-start.9 = (bf16[256,4096]{1,0:T(8,128)(2,1)}, bf16[256,4096]{1,0:T(8,128)(2,1)S(1)}, u32[]{:S(2)}, u32[]{:S(2)}) collective-permute-start(bf16[256,4096]{1,0:T(8,128)(2,1)} %refs_8_.1), channel_id=1, source_target_pairs={{0,1},{1,0},{2,3},{3,2},{4,5},{5,4},{6,7},{7,6},{8,9},{9,8},{10,11... | collective-permute-start | bytes 6291464 | tf_op jit(solution)/shard_map/ppermute | solution.py:262
  3.0 9.6 %collective-permute-start = (bf16[128,256]{1,0:T(8,128)(2,1)S(1)}, bf16[128,256]{1,0:T(8,128)(2,1)S(1)}, u32[]{:S(2)}, u32[]{:S(2)}) collective-permute-start(bf16[128,256]{1,0:T(8,128)(2,1)S(1)} %bitcast.30), channel_id=1, source_target_pairs={{0,1},{1,0},{2,3},{3,2},{4,5},{5,4},{6,7},{7,6},{8,9},{9,8},{10,11... | collective-permute-start | bytes 196616 | tf_op jit(solution)/shard_map/ppermute | solution.py:262
  4.0 9.5 %collective-permute-start.1 = (bf16[256,256]{1,0:T(8,128)(2,1)S(1)}, bf16[256,256]{1,0:T(8,128)(2,1)S(1)}, u32[]{:S(2)}, u32[]{:S(2)}) collective-permute-start(bf16[256,256]{1,0:T(8,128)(2,1)S(1)} %pad_maximum_fusion), channel_id=1, source_target_pairs={{0,0},{1,16},{16,1},{17,17},{32,32},{33,48},{48,33},{49,49},{64,64... | collective-permute-start | bytes 393224 | tf_op jit(solution)/shard_map/ppermute | solution.py:275
  7.7 7.0 %collective-permute-start.2 = (bf16[256,256]{1,0:T(8,128)(2,1)S(1)}, bf16[256,256]{1,0:T(8,128)(2,1)S(1)}, u32[]{:S(2)}, u32[]{:S(2)}) collective-permute-start(bf16[256,256]{1,0:T(8,128)(2,1)S(1)} %pad_maximum_fusion), channel_id=1, source_target_pairs={{0,32},{1,48},{16,33},{17,49},{32,64},{33,80},{48,65},{49,81},{64,... | collective-permute-start | bytes 393224 | tf_op jit(solution)/shard_map/ppermute | solution.py:275
  8.8 8.0 %collective-permute-start.3 = (bf16[256,256]{1,0:T(8,128)(2,1)S(1)}, bf16[256,256]{1,0:T(8,128)(2,1)S(1)}, u32[]{:S(2)}, u32[]{:S(2)}) collective-permute-start(bf16[256,256]{1,0:T(8,128)(2,1)S(1)} %pad_maximum_fusion), channel_id=1, source_target_pairs={{0,64},{1,80},{16,65},{17,81},{32,96},{33,112},{48,97},{49,113},{6... | collective-permute-start | bytes 393224 | tf_op jit(solution)/shard_map/ppermute | solution.py:275
  12.6 5.5 %collective-permute-start.4 = (bf16[256,256]{1,0:T(8,128)(2,1)S(1)}, bf16[256,256]{1,0:T(8,128)(2,1)S(1)}, u32[]{:S(2)}, u32[]{:S(2)}) collective-permute-start(bf16[256,256]{1,0:T(8,128)(2,1)S(1)} %pad_maximum_fusion), channel_id=1, source_target_pairs={{0,96},{1,112},{16,97},{17,113},{32,0},{33,16},{48,1},{49,17},{64,... | collective-permute-start | bytes 393224 | tf_op jit(solution)/shard_map/ppermute | solution.py:275
  13.6 4.6 %collective-permute-start.5 = (bf16[256,256]{1,0:T(8,128)(2,1)S(1)}, bf16[256,256]{1,0:T(8,128)(2,1)S(1)}, u32[]{:S(2)}, u32[]{:S(2)}) collective-permute-start(bf16[256,256]{1,0:T(8,128)(2,1)S(1)} %collective-permute-done.1.refs_0_), channel_id=1, source_target_pairs={{0,1},{1,0},{2,3},{3,2},{4,5},{5,4},{6,7},{7,6},{8,9},{9,8},{10,11... | collective-permute-start | bytes 393224 | tf_op jit(solution)/shard_map/ppermute | solution.py:262
  14.7 3.4 %collective-permute-start.6 = (bf16[256,256]{1,0:T(8,128)(2,1)S(1)}, bf16[256,256]{1,0:T(8,128)(2,1)S(1)}, u32[]{:S(2)}, u32[]{:S(2)}) collective-permute-start(bf16[256,256]{1,0:T(8,128)(2,1)S(1)} %collective-permute-done.2.refs_1_), channel_id=1, source_target_pairs={{0,1},{1,0},{2,3},{3,2},{4,5},{5,4},{6,7},{7,6},{8,9},{9,8},{10,11... | collective-permute-start | bytes 393224 | tf_op jit(solution)/shard_map/ppermute | solution.py:262
  16.8 1.4 collective-permute-start.7
  18.1 1.3 collective-permute-start.8
  19.4 1.6 %copy-start = (bf16[256,4096]{1,0:T(8,128)(2,1)S(1)}, bf16[256,4096]{1,0:T(8,128)(2,1)}, u32[]{:S(2)}) copy-start(bf16[256,4096]{1,0:T(8,128)(2,1)} %refs_8_.1) | copy-start | bytes 6291460
  24.4 7.6 %copy-start.5 = (s32[16,8]{0,1:T(8,128)S(1)}, s32[16,8]{0,1:T(8,128)}, u32[]{:S(2)}) copy-start(s32[16,8]{0,1:T(8,128)} %param.17) | copy-start | bytes 1540
  24.4 22.3 %copy-start.1 = (bf16[16,4096]{1,0:T(8,128)(2,1)S(1)}, bf16[16,4096]{1,0:T(8,128)(2,1)}, u32[]{:S(2)}) copy-start(bf16[16,4096]{1,0:T(8,128)(2,1)} %residual.1) | copy-start | bytes 393220
  24.4 22.3 %copy-start.4 = (f32[4096]{0:T(1024)S(1)}, f32[4096]{0:T(1024)}, u32[]{:S(2)}) copy-start(f32[4096]{0:T(1024)} %param.16) | copy-start | bytes 49156
  24.5 22.3 %all-to-all-start = ((bf16[8,16,4096]{2,1,0:T(8,128)(2,1)}), bf16[8,16,4096]{2,1,0:T(8,128)(2,1)S(1)}, u32[]{:S(2)}, u32[]{:S(2)}) async-start(bf16[8,16,4096]{2,1,0:T(8,128)(2,1)} %bitcast.13), calls=%async_computation | async-start | bytes 2097152 | tf_op jit(solution)/shard_map/all_to_all | solution.py:336
  46.7 0.7 copy-start.2
  103.4 5.0 %copy-start.6 = (f32[16,8]{0,1:T(8,128)S(1)}, f32[16,8]{0,1:T(8,128)}, u32[]{:S(2)}) copy-start(f32[16,8]{0,1:T(8,128)} %param.18) | copy-start | bytes 1540
  103.4 34.7 %copy-start.3 = (s32[16,8]{1,0:T(8,128)S(1)}, s32[16,8]{1,0:T(8,128)}, u32[]{:S(2)}) copy-start(s32[16,8]{1,0:T(8,128)} %number_slots.1.listed.slots) | copy-start | bytes 1540
  103.4 34.7 %all-to-all-start.2 = ((bf16[128,64,128]{2,1,0:T(8,128)(2,1)}), bf16[128,64,128]{2,1,0:T(8,128)(2,1)S(1)}, u32[]{:S(2)}, u32[]{:S(2)}) async-start(bf16[128,64,128]{2,1,0:T(8,128)(2,1)} %bitcast.27), calls=%async_computation.2 | async-start | bytes 4194304 | tf_op jit(solution)/shard_map/all_to_all | solution.py:379

commit v3 on v2

--- a/solution.py
+++ b/solution.py
@@ -26,7 +26,7 @@
 
 VMEM = pl.BlockSpec(memory_space=pltpu.VMEM)
 SMEM = pl.BlockSpec(memory_space=pltpu.SMEM)
-HBM = pl.BlockSpec(memory_space=pltpu.HBM)
+HBM = pl.BlockSpec(memory_space=pl.ANY)
 
 
 def attention_kernel(place, own_queries, twin_queries, *refs):
@@ -106,7 +106,7 @@
         ).astype(jnp.bfloat16)
 
 
-def slots_kernel(routes, slots, counts):
+def slots_kernel(routes, weights, listed, weighed, slots, held, counts, sems):
     @pl.loop(0, EXPERTS)
     def clear(expert):
         counts[expert] = 0
@@ -118,6 +118,16 @@
             rank = counts[expert]
             counts[expert] = rank + 1
             slots[token, choice] = expert * CAP + rank
+            held[token, choice] = weights[token, choice]
+
+    copies = [
+        pltpu.make_async_copy(slots, listed, sems.at[0]),
+        pltpu.make_async_copy(held, weighed, sems.at[1]),
+    ]
+    for copy in copies:
+        copy.start()
+    for copy in copies:
+        copy.wait()
 
 
 def norm_kernel(listed, shares, residual, gain, hidden, outgoing, rows, slots, sem):
@@ -182,8 +192,7 @@
 
     pairs = [pair(part) for part in range(4)]
     downs = [down(part) for part in range(4)]
-    then = [pairs[2], pairs[3], downs[0:2], downs[2:4]]
-    for copy in pairs[0] + pairs[1]:
+    for copy in pairs[0] + pairs[1] + pairs[2] + pairs[3] + downs:
         copy.start()
 
     @pl.loop(0, SLOTS // 32)
@@ -192,16 +201,14 @@
             pl.ds(group * 32 * PIECES, 32 * PIECES), :
         ].astype(jnp.float32)
 
+    for piece in range(PIECES):
+        rows[:, piece * 128 : (piece + 1) * 128] = wide[
+            pl.ds(piece, SLOTS, stride=PIECES), :
+        ].astype(jnp.bfloat16)
     for part in range(4):
-        for piece in range(part * 8, part * 8 + 8):
-            rows[:, piece * 128 : (piece + 1) * 128] = wide[
-                pl.ds(piece, SLOTS, stride=PIECES), :
-            ].astype(jnp.bfloat16)
         span = slice(part * 1024, (part + 1) * 1024)
         for copy in pairs[part]:
             copy.wait()
-        for copy in then[part]:
-            copy.start()
         for total, weights in ((gate, gate_buf), (upward, up_buf)):
             product = jnp.dot(rows[:, span], weights[span, :], preferred_element_type=jnp.float32)
             if part:
@@ -305,14 +312,22 @@
     twin_queries = swap_cores(sent_queries)
     twin_proj = swap_cores(out_proj)
 
-    slots = pl.pallas_call(
+    slots, weights = pl.pallas_call(
         slots_kernel,
-        out_shape=jax.ShapeDtypeStruct((TOKENS, TOP), jnp.int32),
-        in_specs=[SMEM],
-        out_specs=SMEM,
-        scratch_shapes=[pltpu.SMEM((EXPERTS,), jnp.int32)],
+        out_shape=(
+            jax.ShapeDtypeStruct((TOKENS, TOP), jnp.int32),
+            jax.ShapeDtypeStruct((TOKENS, TOP), jnp.float32),
+        ),
+        in_specs=[SMEM, SMEM],
+        out_specs=(HBM, HBM),
+        scratch_shapes=[
+            pltpu.SMEM((TOKENS, TOP), jnp.int32),
+            pltpu.SMEM((TOKENS, TOP), jnp.float32),
+            pltpu.SMEM((EXPERTS,), jnp.int32),
+            pltpu.SemaphoreType.DMA((2,)),
+        ],
         name="number_slots",
-    )(routes)
+    )(routes, route_weights)
 
     place = jnp.stack([ctx_index, core] + origins).astype(jnp.int32)
     partial = pl.pallas_call(
@@ -387,7 +402,7 @@
         scratch_shapes=[pltpu.VMEM((TOKENS * PIECES, 128), jnp.float32)],
         compiler_params=pltpu.CompilerParams(vmem_limit_bytes=16 * MIB),
         name="mix",
-    )(slots, route_weights, returned.reshape(SLOTS, PIECES, 128))
+    )(slots, weights, returned.reshape(SLOTS, PIECES, 128))
     return (hidden_state, expert_mix)
 
 

time: 141 us -> 140 us (level)
  blocking collectives: 40.2 us -> 74.6 us
  waiting for transfers between devices: 46.5 us -> 16.6 us
  starting transfers between devices: 23.6 us -> 18.3 us
    all_to_all x0 -> x1, blocking collectives: none -> 34.9 us  [on_device(): lax.all_to_all(produced.reshape(EXPERTS, CAP * PIECES, 128), ALL, split_a...]
    all_to_all x1 -> x0, waiting for transfers between devices: 29.6 us -> none  [on_device(): lax.all_to_all(produced.reshape(EXPERTS, CAP * PIECES, 128), ALL, split_a...]
    all_to_all x1 -> x0, starting transfers between devices: 4.93 us -> none  [on_device(): lax.all_to_all(produced.reshape(EXPERTS, CAP * PIECES, 128), ALL, split_a...]
    unnamed x16 -> x18, local copies, waits for them, and re-layouts: 3.06 us -> 3.66 us
  transfers between devices with their start and end apart: 12 -> 11, of which waited for: 6 -> 7; matrix products, arithmetic and copies ran while one was open for 2% -> 2% of each run, Pallas kernels for 2% -> 2%
where the time goes in v3:
time: 140 us; the launch traced here: 139 us
  blocking collectives  74.6 us (53%)
  Pallas kernels  23.8 us (17%)
  starting transfers between devices  18.3 us (13%)
  waiting for transfers between devices  16.6 us (12%)
  local copies, waits for them, and re-layouts  5.52 us (4%)
    all_to_all x1, blocking collectives, on_device(): lax.all_to_all(outgoing.reshape(EXPERTS, CAP * PIECES, 128), ALL, split_a...  39.7 us
    all_to_all x1, blocking collectives, on_device(): lax.all_to_all(produced.reshape(EXPERTS, CAP * PIECES, 128), ALL, split_a...  34.9 us
    pallas_call x1, Pallas kernels, on_device(): pl.pallas_call(expert_kernel, out_shape=pltpu.HBM((SLOTS * PIECES, 128),...  13.6 us
    all_to_all x1, waiting for transfers between devices, on_device(): lax.all_to_all(partial.reshape(8, TOKENS, D), CHIPS, split_axis=0, concat...  10.2 us
    ppermute x4, starting transfers between devices, gather_blocks(): fetched.append(lax.ppermute(block, ('x', 'yl', 'c'), pairs))  8.29 us
    all_to_all x1, starting transfers between devices, on_device(): lax.all_to_all(partial.reshape(8, TOKENS, D), CHIPS, split_axis=0, concat...  7.65 us
    ppermute x4, waiting for transfers between devices, gather_blocks(): fetched.append(lax.ppermute(block, ('x', 'yl', 'c'), pairs))  5.12 us
    unnamed x18, local copies, waits for them, and re-layouts  3.66 us
  transfers between devices with their start and end apart: 11, of which 7 were waited for; matrix products, arithmetic and copies ran while one was open for 2% of the time, Pallas kernels for 2%

profile of v3, /device:TPU:1, one launch (start us, length us, event | category | flops | bytes accessed | tf_op | source)
XLA Modules:
  0.0 139.5 jit_solution(7100364871087151707)
XLA Ops:
  0.6 1.5 %collective-permute-start.9 = (bf16[256,4096]{1,0:T(8,128)(2,1)}, bf16[256,4096]{1,0:T(8,128)(2,1)S(1)}, u32[]{:S(2)}, u32[]{:S(2)}) collective-permute-start(bf16[256,4096]{1,0:T(8,128)(2,1)} %refs_8_.1), channel_id=1, source_target_pairs={{0,1},{1,0},{2,3},{3,2},{4,5},{5,4},{6,7},{7,6},{8,9},{9,8},{10,11... | collective-permute-start | bytes 6291464 | tf_op jit(solution)/shard_map/ppermute | solution.py:269
  2.1 0.9 constant_dynamic-slice_fusion.2
  3.0 0.1 collective-permute-start
  3.1 0.9 constant_dynamic-slice_fusion
  4.0 4.0 %collective-permute-start.4 = (bf16[256,256]{1,0:T(8,128)(2,1)S(1)}, bf16[256,256]{1,0:T(8,128)(2,1)S(1)}, u32[]{:S(2)}, u32[]{:S(2)}) collective-permute-start(bf16[256,256]{1,0:T(8,128)(2,1)S(1)} %pad_maximum_fusion), channel_id=1, source_target_pairs={{0,96},{1,112},{16,97},{17,113},{32,0},{33,16},{48,1},{49,17},{64,... | collective-permute-start | bytes 393224 | tf_op jit(solution)/shard_map/ppermute | solution.py:282
  8.0 0.4 collective-permute-start.3
  8.4 1.9 %collective-permute-start.2 = (bf16[256,256]{1,0:T(8,128)(2,1)S(1)}, bf16[256,256]{1,0:T(8,128)(2,1)S(1)}, u32[]{:S(2)}, u32[]{:S(2)}) collective-permute-start(bf16[256,256]{1,0:T(8,128)(2,1)S(1)} %pad_maximum_fusion), channel_id=1, source_target_pairs={{0,32},{1,48},{16,33},{17,49},{32,64},{33,80},{48,65},{49,81},{64,... | collective-permute-start | bytes 393224 | tf_op jit(solution)/shard_map/ppermute | solution.py:282
  10.3 0.0 collective-permute-done.twin_queries
  10.4 2.0 %collective-permute-start.1 = (bf16[256,256]{1,0:T(8,128)(2,1)S(1)}, bf16[256,256]{1,0:T(8,128)(2,1)S(1)}, u32[]{:S(2)}, u32[]{:S(2)}) collective-permute-start(bf16[256,256]{1,0:T(8,128)(2,1)S(1)} %pad_maximum_fusion), channel_id=1, source_target_pairs={{0,0},{1,16},{16,1},{17,17},{32,32},{33,48},{48,33},{49,49},{64,64... | collective-permute-start | bytes 393224 | tf_op jit(solution)/shard_map/ppermute | solution.py:282
  12.4 1.4 collective-permute-done.4.refs_3_
  13.7 0.0 collective-permute-start.8
  13.7 2.2 %collective-permute-done.3.refs_2_ = bf16[256,256]{1,0:T(8,128)(2,1)S(1)} collective-permute-done((bf16[256,256]{1,0:T(8,128)(2,1)S(1)}, bf16[256,256]{1,0:T(8,128)(2,1)S(1)}, u32[]{:S(2)}, u32[]{:S(2)}) %collective-permute-start.3) | collective-permute-done | bytes 131104 | tf_op jit(solution)/shard_map/ppermute | solution.py:282
  15.9 0.0 collective-permute-start.7
  15.9 1.4 collective-permute-done.2.refs_1_
  17.3 0.7 collective-permute-start.6
  18.0 0.2 collective-permute-done.1.refs_0_
  18.2 0.0 collective-permute-start.5
  18.2 0.1 stack.43.place
  18.3 0.0 collective-permute-done.8.refs_7_
  18.3 0.0 collective-permute-done.7.refs_6_
  18.3 0.7 collective-permute-done.6.refs_5_
  19.0 0.6 collective-permute-done.5.refs_4_
  19.5 0.0 collective-permute-done.9.refs_9_
  19.5 0.0 copy-start
  19.5 1.6 %copy-done = bf16[256,4096]{1,0:T(8,128)(2,1)S(1)} copy-done((bf16[256,4096]{1,0:T(8,128)(2,1)S(1)}, bf16[256,4096]{1,0:T(8,128)(2,1)}, u32[]{:S(2)}) %copy-start) | copy-done | bytes 2097176
  21.1 3.4 %attend_project.1 = bf16[128,4096]{1,0:T(8,128)(2,1)} custom-call(s32[10]{0:T(128)S(1)} %stack.43.place, bf16[128,256]{1,0:T(8,128)(2,1)S(1)} %bitcast.25, bf16[128,256]{1,0:T(8,128)(2,1)S(1)} %collective-permute-done.twin_queries, bf16[256,256]{1,0:T(8,128)(2,1)S(1)} %collective-permute-done.1.refs_0_, bf16[256,256]{1,0:T(8,128)(2,1)S(1)} %collective-permute-done.2.refs_1_, ...), custom_call_target="tpu_custom_call" | custom-call | tf_op jit(solution)/shard_map/attend_project/pallas_call | solution.py:333
  24.5 0.0 copy-start.6
  24.5 0.0 copy-start.7
  24.6 0.0 copy-start.1
  24.6 0.0 copy-start.4
  24.6 7.6 %all-to-all-start = ((bf16[8,16,4096]{2,1,0:T(8,128)(2,1)}), bf16[8,16,4096]{2,1,0:T(8,128)(2,1)S(1)}, u32[]{:S(2)}, u32[]{:S(2)}) async-start(bf16[8,16,4096]{2,1,0:T(8,128)(2,1)} %bitcast.13), calls=%async_computation | async-start | bytes 2097152 | tf_op jit(solution)/shard_map/all_to_all | solution.py:351
  32.2 0.0 copy-done.6
  32.2 0.7 copy.13.routes
  32.9 0.0 copy-done.7
  32.9 0.7 copy.14.weights
  33.6 3.2 %number_slots.1 = (s32[16,8]{1,0:T(8,128)}, f32[16,8]{1,0:T(8,128)}) custom-call(s32[16,8]{1,0:T(8,128)} %copy.13.routes, f32[16,8]{1,0:T(8,128)} %copy.14.weights), custom_call_target="tpu_custom_call" | custom-call | tf_op jit(solution)/shard_map/number_slots/pallas_call | solution.py:315
  36.8 10.2 %all-to-all-done.shares = bf16[8,16,4096]{2,1,0:T(8,128)(2,1)S(1)} async-done(((bf16[8,16,4096]{2,1,0:T(8,128)(2,1)}), bf16[8,16,4096]{2,1,0:T(8,128)(2,1)S(1)}, u32[]{:S(2)}, u32[]{:S(2)}) %all-to-all-start) | async-done | bytes 1048608 | tf_op jit(solution)/shard_map/all_to_all | solution.py:351
  47.0 0.0 copy-done.1
  47.0 0.0 copy-done.4
  47.0 0.0 copy-start.2
  47.0 0.7 copy-done.2
  47.7 1.6 %norm_dispatch.1 = (bf16[16,4096]{1,0:T(8,128)(2,1)}, bf16[256,32,128]{2,1,0:T(8,128)(2,1)S(1)}) custom-call(s32[16,8]{1,0:T(8,128)S(1)} %copy-done.2, bf16[8,16,4096]{2,1,0:T(8,128)(2,1)S(1)} %all-to-all-done.shares, bf16[16,4096]{1,0:T(8,128)(2,1)S(1)} %copy-done.1, f32[1,4096]{1,0:T(1,128)S(1)} %bitcast.26), custom_call_target="tpu_custom_call" | custom-call | tf_op jit(solution)/shard_map/norm_dispatch/pallas_call | solution.py:354
  49.3 39.7 %all_to_all.15 = bf16[128,64,128]{2,1,0:T(8,128)(2,1)} all-to-all(bf16[128,64,128]{2,1,0:T(8,128)(2,1)S(1)} %bitcast.24), channel_id=1, replica_groups=mesh['x'=4,'yl'=2,'yh'=2,'z'=4,'c'=2] {'x','yl','yh','z','c'}, dimensions={0} | all-to-all | bytes 4194304 | tf_op jit(solution)/shard_map/all_to_all | solution.py:371
  89.0 13.6 %expert_rows.1 = bf16[8192,128]{1,0:T(8,128)(2,1)} custom-call(bf16[8192,128]{1,0:T(8,128)(2,1)} %bitcast.27, bf16[1,4096,768]{2,1,0:T(8,128)(2,1)} %w_gate.1, bf16[1,4096,768]{2,1,0:T(8,128)(2,1)} %w_up.1, bf16[1,768,4096]{2,1,0:T(8,128)(2,1)} %w_down.1), custom_call_target="tpu_custom_call" | custom-call | tf_op jit(solution)/shard_map/expert_rows/pallas_call | solution.py:374
  102.6 0.0 copy-start.3
  102.6 0.0 copy-start.5
  102.6 34.9 %all_to_all.16 = bf16[128,64,128]{2,1,0:T(8,128)(2,1)S(1)} all-to-all(bf16[128,64,128]{2,1,0:T(8,128)(2,1)} %bitcast.28), channel_id=1, replica_groups=mesh['x'=4,'yl'=2,'yh'=2,'z'=4,'c'=2] {'x','yl','yh','z','c'}, dimensions={0} | all-to-all | bytes 4194304 | tf_op jit(solution)/shard_map/all_to_all | solution.py:394
  137.4 0.0 copy-done.3
  137.4 0.0 copy-done.5
  137.5 2.0 %mix.1 = f32[16,4096]{1,0:T(8,128)} custom-call(s32[16,8]{1,0:T(8,128)S(1)} %copy-done.3, f32[16,8]{1,0:T(8,128)S(1)} %copy-done.5, bf16[256,32,128]{2,1,0:T(8,128)(2,1)S(1)} %bitcast.23), custom_call_target="tpu_custom_call" | custom-call | tf_op jit(solution)/shard_map/mix/pallas_call | solution.py:397
  (1 shorter events, 0.0 us)
Async XLA Ops:
  0.6 18.9 %collective-permute-start.9 = (bf16[256,4096]{1,0:T(8,128)(2,1)}, bf16[256,4096]{1,0:T(8,128)(2,1)S(1)}, u32[]{:S(2)}, u32[]{:S(2)}) collective-permute-start(bf16[256,4096]{1,0:T(8,128)(2,1)} %refs_8_.1), channel_id=1, source_target_pairs={{0,1},{1,0},{2,3},{3,2},{4,5},{5,4},{6,7},{7,6},{8,9},{9,8},{10,11... | collective-permute-start | bytes 6291464 | tf_op jit(solution)/shard_map/ppermute | solution.py:269
  3.0 7.3 %collective-permute-start = (bf16[128,256]{1,0:T(8,128)(2,1)S(1)}, bf16[128,256]{1,0:T(8,128)(2,1)S(1)}, u32[]{:S(2)}, u32[]{:S(2)}) collective-permute-start(bf16[128,256]{1,0:T(8,128)(2,1)S(1)} %bitcast.30), channel_id=1, source_target_pairs={{0,1},{1,0},{2,3},{3,2},{4,5},{5,4},{6,7},{7,6},{8,9},{9,8},{10,11... | collective-permute-start | bytes 196616 | tf_op jit(solution)/shard_map/ppermute | solution.py:269
  4.0 9.7 %collective-permute-start.4 = (bf16[256,256]{1,0:T(8,128)(2,1)S(1)}, bf16[256,256]{1,0:T(8,128)(2,1)S(1)}, u32[]{:S(2)}, u32[]{:S(2)}) collective-permute-start(bf16[256,256]{1,0:T(8,128)(2,1)S(1)} %pad_maximum_fusion), channel_id=1, source_target_pairs={{0,96},{1,112},{16,97},{17,113},{32,0},{33,16},{48,1},{49,17},{64,... | collective-permute-start | bytes 393224 | tf_op jit(solution)/shard_map/ppermute | solution.py:282
  8.0 7.9 %collective-permute-start.3 = (bf16[256,256]{1,0:T(8,128)(2,1)S(1)}, bf16[256,256]{1,0:T(8,128)(2,1)S(1)}, u32[]{:S(2)}, u32[]{:S(2)}) collective-permute-start(bf16[256,256]{1,0:T(8,128)(2,1)S(1)} %pad_maximum_fusion), channel_id=1, source_target_pairs={{0,64},{1,80},{16,65},{17,81},{32,96},{33,112},{48,97},{49,113},{6... | collective-permute-start | bytes 393224 | tf_op jit(solution)/shard_map/ppermute | solution.py:282
  8.4 8.9 %collective-permute-start.2 = (bf16[256,256]{1,0:T(8,128)(2,1)S(1)}, bf16[256,256]{1,0:T(8,128)(2,1)S(1)}, u32[]{:S(2)}, u32[]{:S(2)}) collective-permute-start(bf16[256,256]{1,0:T(8,128)(2,1)S(1)} %pad_maximum_fusion), channel_id=1, source_target_pairs={{0,32},{1,48},{16,33},{17,49},{32,64},{33,80},{48,65},{49,81},{64,... | collective-permute-start | bytes 393224 | tf_op jit(solution)/shard_map/ppermute | solution.py:282
  10.4 7.8 %collective-permute-start.1 = (bf16[256,256]{1,0:T(8,128)(2,1)S(1)}, bf16[256,256]{1,0:T(8,128)(2,1)S(1)}, u32[]{:S(2)}, u32[]{:S(2)}) collective-permute-start(bf16[256,256]{1,0:T(8,128)(2,1)S(1)} %pad_maximum_fusion), channel_id=1, source_target_pairs={{0,0},{1,16},{16,1},{17,17},{32,32},{33,48},{48,33},{49,49},{64,64... | collective-permute-start | bytes 393224 | tf_op jit(solution)/shard_map/ppermute | solution.py:282
  13.7 4.5 %collective-permute-start.8 = (bf16[256,256]{1,0:T(8,128)(2,1)S(1)}, bf16[256,256]{1,0:T(8,128)(2,1)S(1)}, u32[]{:S(2)}, u32[]{:S(2)}) collective-permute-start(bf16[256,256]{1,0:T(8,128)(2,1)S(1)} %collective-permute-done.4.refs_3_), channel_id=1, source_target_pairs={{0,1},{1,0},{2,3},{3,2},{4,5},{5,4},{6,7},{7,6},{8,9},{9,8},{10,11... | collective-permute-start | bytes 393224 | tf_op jit(solution)/shard_map/ppermute | solution.py:269
  15.9 2.4 %collective-permute-start.7 = (bf16[256,256]{1,0:T(8,128)(2,1)S(1)}, bf16[256,256]{1,0:T(8,128)(2,1)S(1)}, u32[]{:S(2)}, u32[]{:S(2)}) collective-permute-start(bf16[256,256]{1,0:T(8,128)(2,1)S(1)} %collective-permute-done.3.refs_2_), channel_id=1, source_target_pairs={{0,1},{1,0},{2,3},{3,2},{4,5},{5,4},{6,7},{7,6},{8,9},{9,8},{10,11... | collective-permute-start | bytes 393224 | tf_op jit(solution)/shard_map/ppermute | solution.py:269
  17.3 1.7 %collective-permute-start.6 = (bf16[256,256]{1,0:T(8,128)(2,1)S(1)}, bf16[256,256]{1,0:T(8,128)(2,1)S(1)}, u32[]{:S(2)}, u32[]{:S(2)}) collective-permute-start(bf16[256,256]{1,0:T(8,128)(2,1)S(1)} %collective-permute-done.2.refs_1_), channel_id=1, source_target_pairs={{0,1},{1,0},{2,3},{3,2},{4,5},{5,4},{6,7},{7,6},{8,9},{9,8},{10,11... | collective-permute-start | bytes 393224 | tf_op jit(solution)/shard_map/ppermute | solution.py:269
  18.2 1.3 collective-permute-start.5
  19.5 1.6 %copy-start = (bf16[256,4096]{1,0:T(8,128)(2,1)S(1)}, bf16[256,4096]{1,0:T(8,128)(2,1)}, u32[]{:S(2)}) copy-start(bf16[256,4096]{1,0:T(8,128)(2,1)} %refs_8_.1) | copy-start | bytes 6291460
  24.5 7.7 %copy-start.6 = (s32[16,8]{0,1:T(8,128)S(1)}, s32[16,8]{0,1:T(8,128)}, u32[]{:S(2)}) copy-start(s32[16,8]{0,1:T(8,128)} %param.17) | copy-start | bytes 1540
  24.5 8.4 %copy-start.7 = (f32[16,8]{0,1:T(8,128)S(1)}, f32[16,8]{0,1:T(8,128)}, u32[]{:S(2)}) copy-start(f32[16,8]{0,1:T(8,128)} %param.18) | copy-start | bytes 1540
  24.6 22.4 %copy-start.1 = (bf16[16,4096]{1,0:T(8,128)(2,1)S(1)}, bf16[16,4096]{1,0:T(8,128)(2,1)}, u32[]{:S(2)}) copy-start(bf16[16,4096]{1,0:T(8,128)(2,1)} %residual.1) | copy-start | bytes 393220
  24.6 22.4 %copy-start.4 = (f32[4096]{0:T(1024)S(1)}, f32[4096]{0:T(1024)}, u32[]{:S(2)}) copy-start(f32[4096]{0:T(1024)} %param.16) | copy-start | bytes 49156
  24.6 22.4 %all-to-all-start = ((bf16[8,16,4096]{2,1,0:T(8,128)(2,1)}), bf16[8,16,4096]{2,1,0:T(8,128)(2,1)S(1)}, u32[]{:S(2)}, u32[]{:S(2)}) async-start(bf16[8,16,4096]{2,1,0:T(8,128)(2,1)} %bitcast.13), calls=%async_computation | async-start | bytes 2097152 | tf_op jit(solution)/shard_map/all_to_all | solution.py:351
  47.0 0.7 copy-start.2
  102.6 34.9 %copy-start.3 = (s32[16,8]{1,0:T(8,128)S(1)}, s32[16,8]{1,0:T(8,128)}, u32[]{:S(2)}) copy-start(s32[16,8]{1,0:T(8,128)} %get-tuple-element.6.listed.slots) | copy-start | bytes 1540
  102.6 34.9 %copy-start.5 = (f32[16,8]{1,0:T(8,128)S(1)}, f32[16,8]{1,0:T(8,128)}, u32[]{:S(2)}) copy-start(f32[16,8]{1,0:T(8,128)} %get-tuple-element.8.weights) | copy-start | bytes 1540

commit v4 on v3

--- a/solution.py
+++ b/solution.py
@@ -311,6 +311,8 @@
     sent_queries = lax.dynamic_index_in_dim(split, 1 - core, 1, False).reshape(128, 256)
     twin_queries = swap_cores(sent_queries)
     twin_proj = swap_cores(out_proj)
+    sent_back, blocks[0] = lax.optimization_barrier((twin_proj, blocks[0]))
+    own_proj = swap_cores(sent_back)
 
     slots, weights = pl.pallas_call(
         slots_kernel,
@@ -346,7 +348,7 @@
         ],
         compiler_params=pltpu.CompilerParams(vmem_limit_bytes=24 * MIB),
         name="attend_project",
-    )(place, own_queries, twin_queries, *blocks, out_proj, twin_proj)
+    )(place, own_queries, twin_queries, *blocks, own_proj, twin_proj)
 
     shares = lax.all_to_all(
         partial.reshape(8, TOKENS, D), CHIPS, split_axis=0, concat_axis=0, tiled=True

time: 140 us -> 142 us (1.014)
  starting transfers between devices: 18.3 us -> 20.5 us
  local copies, waits for them, and re-layouts: 5.52 us -> 3.92 us
    ppermute x4, starting transfers between devices: 8.29 us -> 10.2 us  [gather_blocks(): fetched.append(lax.ppermute(block, ('x', 'yl', 'c'), pairs))]
    unnamed x18 -> x16, local copies, waits for them, and re-layouts: 3.66 us -> 2.07 us
  transfers between devices with their start and end apart: 11 -> 12, of which waited for: 7 -> 6; matrix products, arithmetic and copies ran while one was open for 2% -> 2% of each run, Pallas kernels for 2% -> 2%
where the time goes in v4:
time: 142 us
  blocking collectives  74.9 us (53%)
  Pallas kernels  24.3 us (17%)
  starting transfers between devices  20.5 us (14%)
  waiting for transfers between devices  17.4 us (12%)
  local copies, waits for them, and re-layouts  3.92 us (3%)
    all_to_all x1, blocking collectives, on_device(): lax.all_to_all(outgoing.reshape(EXPERTS, CAP * PIECES, 128), ALL, split_a...  40.1 us
    all_to_all x1, blocking collectives, on_device(): lax.all_to_all(produced.reshape(EXPERTS, CAP * PIECES, 128), ALL, split_a...  34.9 us
    pallas_call x1, Pallas kernels, on_device(): pl.pallas_call(expert_kernel, out_shape=pltpu.HBM((SLOTS * PIECES, 128),...  13.6 us
    ppermute x4, starting transfers between devices, gather_blocks(): fetched.append(lax.ppermute(block, ('x', 'yl', 'c'), pairs))  10.2 us
    all_to_all x1, waiting for transfers between devices, on_device(): lax.all_to_all(partial.reshape(8, TOKENS, D), CHIPS, split_axis=0, concat...  10 us
    all_to_all x1, starting transfers between devices, on_device(): lax.all_to_all(partial.reshape(8, TOKENS, D), CHIPS, split_axis=0, concat...  7.67 us
    ppermute x4, waiting for transfers between devices, gather_blocks(): fetched.append(lax.ppermute(block, ('x', 'yl', 'c'), pairs))  5.15 us
    pallas_call x1, Pallas kernels, on_device(): pl.pallas_call(attention_kernel, out_shape=jax.ShapeDtypeStruct((128, D),...  3.85 us
  transfers between devices with their start and end apart: 12, of which 6 were waited for; matrix products, arithmetic and copies ran while one was open for 2% of the time, Pallas kernels for 2%

profile of v4, /device:TPU:1, one launch (start us, length us, event | category | flops | bytes accessed | tf_op | source)
XLA Modules:
  0.0 141.7 jit_solution(17772527456939207564)
XLA Ops:
  0.6 1.5 %collective-permute-start.1 = (bf16[256,4096]{1,0:T(8,128)(2,1)}, bf16[256,4096]{1,0:T(8,128)(2,1)S(1)}, u32[]{:S(2)}, u32[]{:S(2)}) collective-permute-start(bf16[256,4096]{1,0:T(8,128)(2,1)} %param.14), channel_id=1, source_target_pairs={{0,1},{1,0},{2,3},{3,2},{4,5},{5,4},{6,7},{7,6},{8,9},{9,8},{10,11... | collective-permute-start | bytes 6291464 | tf_op jit(solution)/shard_map/ppermute | solution.py:269
  2.1 0.9 constant_dynamic-slice_fusion
  3.0 3.2 %collective-permute-start.2 = (bf16[256,256]{1,0:T(8,128)(2,1)S(1)}, bf16[256,256]{1,0:T(8,128)(2,1)S(1)}, u32[]{:S(2)}, u32[]{:S(2)}) collective-permute-start(bf16[256,256]{1,0:T(8,128)(2,1)S(1)} %pad_maximum_fusion), channel_id=1, source_target_pairs={{0,0},{1,16},{16,1},{17,17},{32,32},{33,48},{48,33},{49,49},{64,64... | collective-permute-start | bytes 393224 | tf_op jit(solution)/shard_map/ppermute | solution.py:282
  6.3 3.1 %collective-permute-done.2.refs_0_ = bf16[256,256]{1,0:T(8,128)(2,1)S(1)} collective-permute-done((bf16[256,256]{1,0:T(8,128)(2,1)S(1)}, bf16[256,256]{1,0:T(8,128)(2,1)S(1)}, u32[]{:S(2)}, u32[]{:S(2)}) %collective-permute-start.2) | collective-permute-done | bytes 131104 | tf_op jit(solution)/shard_map/ppermute | solution.py:282
  9.3 0.0 collective-permute-done.1.refs_9_
  9.3 0.0 collective-permute-start.10
  9.3 2.2 %collective-permute-start.3 = (bf16[256,256]{1,0:T(8,128)(2,1)S(1)}, bf16[256,256]{1,0:T(8,128)(2,1)S(1)}, u32[]{:S(2)}, u32[]{:S(2)}) collective-permute-start(bf16[256,256]{1,0:T(8,128)(2,1)S(1)} %pad_maximum_fusion), channel_id=1, source_target_pairs={{0,32},{1,48},{16,33},{17,49},{32,64},{33,80},{48,65},{49,81},{64,... | collective-permute-start | bytes 393224 | tf_op jit(solution)/shard_map/ppermute | solution.py:282
  11.6 2.7 %collective-permute-start.4 = (bf16[256,256]{1,0:T(8,128)(2,1)S(1)}, bf16[256,256]{1,0:T(8,128)(2,1)S(1)}, u32[]{:S(2)}, u32[]{:S(2)}) collective-permute-start(bf16[256,256]{1,0:T(8,128)(2,1)S(1)} %pad_maximum_fusion), channel_id=1, source_target_pairs={{0,64},{1,80},{16,65},{17,81},{32,96},{33,112},{48,97},{49,113},{6... | collective-permute-start | bytes 393224 | tf_op jit(solution)/shard_map/ppermute | solution.py:282
  14.3 2.1 %collective-permute-start.5 = (bf16[256,256]{1,0:T(8,128)(2,1)S(1)}, bf16[256,256]{1,0:T(8,128)(2,1)S(1)}, u32[]{:S(2)}, u32[]{:S(2)}) collective-permute-start(bf16[256,256]{1,0:T(8,128)(2,1)S(1)} %pad_maximum_fusion), channel_id=1, source_target_pairs={{0,96},{1,112},{16,97},{17,113},{32,0},{33,16},{48,1},{49,17},{64,... | collective-permute-start | bytes 393224 | tf_op jit(solution)/shard_map/ppermute | solution.py:282
  16.4 0.9 constant_dynamic-slice_fusion.2
  17.2 0.1 collective-permute-start
  17.3 1.2 collective-permute-done.twin_queries
  18.6 0.2 collective-permute-start.6
  18.7 0.0 collective-permute-done.3.refs_1_
  18.7 0.4 collective-permute-start.7
  19.1 2.1 %collective-permute-done.4.refs_2_ = bf16[256,256]{1,0:T(8,128)(2,1)S(1)} collective-permute-done((bf16[256,256]{1,0:T(8,128)(2,1)S(1)}, bf16[256,256]{1,0:T(8,128)(2,1)S(1)}, u32[]{:S(2)}, u32[]{:S(2)}) %collective-permute-start.4) | collective-permute-done | bytes 131104 | tf_op jit(solution)/shard_map/ppermute | solution.py:282
  21.2 0.1 collective-permute-start.8
  21.3 0.0 collective-permute-done.5.refs_3_
  21.3 0.4 collective-permute-start.9
  21.7 0.1 stack.43.place
  21.8 0.0 collective-permute-done.6.refs_4_
  21.8 0.0 collective-permute-done.7.refs_5_
  21.8 0.7 collective-permute-done.8.refs_6_
  22.5 0.2 collective-permute-done.9.refs_7_
  22.7 0.0 collective-permute-done.10.refs_8_
  22.7 3.9 %attend_project.1 = bf16[128,4096]{1,0:T(8,128)(2,1)} custom-call(s32[10]{0:T(128)S(1)} %stack.43.place, bf16[128,256]{1,0:T(8,128)(2,1)S(1)} %bitcast.25, bf16[128,256]{1,0:T(8,128)(2,1)S(1)} %collective-permute-done.twin_queries, bf16[256,256]{1,0:T(8,128)(2,1)S(1)} %collective-permute-done.2.refs_0_, bf16[256,256]{1,0:T(8,128)(2,1)S(1)} %collective-permute-done.3.refs_1_, ...), custom_call_target="tpu_custom_call" | custom-call | tf_op jit(solution)/shard_map/attend_project/pallas_call | solution.py:335
  26.6 0.0 copy-start.5
  26.6 0.0 copy-start.6
  26.6 0.0 copy-start
  26.6 0.0 copy-start.3
  26.6 7.7 %all-to-all-start = ((bf16[8,16,4096]{2,1,0:T(8,128)(2,1)}), bf16[8,16,4096]{2,1,0:T(8,128)(2,1)S(1)}, u32[]{:S(2)}, u32[]{:S(2)}) async-start(bf16[8,16,4096]{2,1,0:T(8,128)(2,1)} %bitcast.13), calls=%async_computation | async-start | bytes 2097152 | tf_op jit(solution)/shard_map/all_to_all | solution.py:353
  34.3 0.0 copy-done.5
  34.3 0.7 copy.13.routes
  35.0 0.0 copy-done.6
  35.0 0.7 copy.14.weights
  35.6 3.2 %number_slots.1 = (s32[16,8]{1,0:T(8,128)}, f32[16,8]{1,0:T(8,128)}) custom-call(s32[16,8]{1,0:T(8,128)} %copy.13.routes, f32[16,8]{1,0:T(8,128)} %copy.14.weights), custom_call_target="tpu_custom_call" | custom-call | tf_op jit(solution)/shard_map/number_slots/pallas_call | solution.py:317
  38.8 10.0 %all-to-all-done.shares = bf16[8,16,4096]{2,1,0:T(8,128)(2,1)S(1)} async-done(((bf16[8,16,4096]{2,1,0:T(8,128)(2,1)}), bf16[8,16,4096]{2,1,0:T(8,128)(2,1)S(1)}, u32[]{:S(2)}, u32[]{:S(2)}) %all-to-all-start) | async-done | bytes 1048608 | tf_op jit(solution)/shard_map/all_to_all | solution.py:353
  48.9 0.0 copy-done
  48.9 0.0 copy-done.3
  48.9 0.0 copy-start.1
  48.9 0.7 copy-done.1
  49.6 1.6 %norm_dispatch.1 = (bf16[16,4096]{1,0:T(8,128)(2,1)}, bf16[256,32,128]{2,1,0:T(8,128)(2,1)S(1)}) custom-call(s32[16,8]{1,0:T(8,128)S(1)} %copy-done.1, bf16[8,16,4096]{2,1,0:T(8,128)(2,1)S(1)} %all-to-all-done.shares, bf16[16,4096]{1,0:T(8,128)(2,1)S(1)} %copy-done, f32[1,4096]{1,0:T(1,128)S(1)} %bitcast.26), custom_call_target="tpu_custom_call" | custom-call | tf_op jit(solution)/shard_map/norm_dispatch/pallas_call | solution.py:356
  51.2 40.1 %all_to_all.15 = bf16[128,64,128]{2,1,0:T(8,128)(2,1)} all-to-all(bf16[128,64,128]{2,1,0:T(8,128)(2,1)S(1)} %bitcast.24), channel_id=1, replica_groups=mesh['x'=4,'yl'=2,'yh'=2,'z'=4,'c'=2] {'x','yl','yh','z','c'}, dimensions={0} | all-to-all | bytes 4194304 | tf_op jit(solution)/shard_map/all_to_all | solution.py:373
  91.2 13.6 %expert_rows.1 = bf16[8192,128]{1,0:T(8,128)(2,1)} custom-call(bf16[8192,128]{1,0:T(8,128)(2,1)} %bitcast.27, bf16[1,4096,768]{2,1,0:T(8,128)(2,1)} %w_gate.1, bf16[1,4096,768]{2,1,0:T(8,128)(2,1)} %w_up.1, bf16[1,768,4096]{2,1,0:T(8,128)(2,1)} %w_down.1), custom_call_target="tpu_custom_call" | custom-call | tf_op jit(solution)/shard_map/expert_rows/pallas_call | solution.py:376
  104.8 0.0 copy-start.2
  104.8 0.0 copy-start.4
  104.8 34.9 %all_to_all.16 = bf16[128,64,128]{2,1,0:T(8,128)(2,1)S(1)} all-to-all(bf16[128,64,128]{2,1,0:T(8,128)(2,1)} %bitcast.28), channel_id=1, replica_groups=mesh['x'=4,'yl'=2,'yh'=2,'z'=4,'c'=2] {'x','yl','yh','z','c'}, dimensions={0} | all-to-all | bytes 4194304 | tf_op jit(solution)/shard_map/all_to_all | solution.py:396
  139.7 0.0 copy-done.2
  139.7 0.0 copy-done.4
  139.7 2.0 %mix.1 = f32[16,4096]{1,0:T(8,128)} custom-call(s32[16,8]{1,0:T(8,128)S(1)} %copy-done.2, f32[16,8]{1,0:T(8,128)S(1)} %copy-done.4, bf16[256,32,128]{2,1,0:T(8,128)(2,1)S(1)} %bitcast.23), custom_call_target="tpu_custom_call" | custom-call | tf_op jit(solution)/shard_map/mix/pallas_call | solution.py:399
  (1 shorter events, 0.0 us)
Async XLA Ops:
  0.6 8.7 %collective-permute-start.1 = (bf16[256,4096]{1,0:T(8,128)(2,1)}, bf16[256,4096]{1,0:T(8,128)(2,1)S(1)}, u32[]{:S(2)}, u32[]{:S(2)}) collective-permute-start(bf16[256,4096]{1,0:T(8,128)(2,1)} %param.14), channel_id=1, source_target_pairs={{0,1},{1,0},{2,3},{3,2},{4,5},{5,4},{6,7},{7,6},{8,9},{9,8},{10,11... | collective-permute-start | bytes 6291464 | tf_op jit(solution)/shard_map/ppermute | solution.py:269
  3.0 6.3 %collective-permute-start.2 = (bf16[256,256]{1,0:T(8,128)(2,1)S(1)}, bf16[256,256]{1,0:T(8,128)(2,1)S(1)}, u32[]{:S(2)}, u32[]{:S(2)}) collective-permute-start(bf16[256,256]{1,0:T(8,128)(2,1)S(1)} %pad_maximum_fusion), channel_id=1, source_target_pairs={{0,0},{1,16},{16,1},{17,17},{32,32},{33,48},{48,33},{49,49},{64,64... | collective-permute-start | bytes 393224 | tf_op jit(solution)/shard_map/ppermute | solution.py:282
  9.3 13.4 %collective-permute-start.10 = (bf16[256,4096]{1,0:T(8,128)(2,1)S(1)}, bf16[256,4096]{1,0:T(8,128)(2,1)}, u32[]{:S(2)}, u32[]{:S(2)}) collective-permute-start(bf16[256,4096]{1,0:T(8,128)(2,1)S(1)} %collective-permute-done.1.refs_9_), channel_id=1, source_target_pairs={{0,1},{1,0},{2,3},{3,2},{4,5},{5,4},{6,7},{7,6},{8,9},{9,8},{10,11... | collective-permute-start | bytes 6291464 | tf_op jit(solution)/shard_map/ppermute | solution.py:269
  9.3 9.4 %collective-permute-start.3 = (bf16[256,256]{1,0:T(8,128)(2,1)S(1)}, bf16[256,256]{1,0:T(8,128)(2,1)S(1)}, u32[]{:S(2)}, u32[]{:S(2)}) collective-permute-start(bf16[256,256]{1,0:T(8,128)(2,1)S(1)} %pad_maximum_fusion), channel_id=1, source_target_pairs={{0,32},{1,48},{16,33},{17,49},{32,64},{33,80},{48,65},{49,81},{64,... | collective-permute-start | bytes 393224 | tf_op jit(solution)/shard_map/ppermute | solution.py:282
  11.6 9.6 %collective-permute-start.4 = (bf16[256,256]{1,0:T(8,128)(2,1)S(1)}, bf16[256,256]{1,0:T(8,128)(2,1)S(1)}, u32[]{:S(2)}, u32[]{:S(2)}) collective-permute-start(bf16[256,256]{1,0:T(8,128)(2,1)S(1)} %pad_maximum_fusion), channel_id=1, source_target_pairs={{0,64},{1,80},{16,65},{17,81},{32,96},{33,112},{48,97},{49,113},{6... | collective-permute-start | bytes 393224 | tf_op jit(solution)/shard_map/ppermute | solution.py:282
  14.3 7.0 %collective-permute-start.5 = (bf16[256,256]{1,0:T(8,128)(2,1)S(1)}, bf16[256,256]{1,0:T(8,128)(2,1)S(1)}, u32[]{:S(2)}, u32[]{:S(2)}) collective-permute-start(bf16[256,256]{1,0:T(8,128)(2,1)S(1)} %pad_maximum_fusion), channel_id=1, source_target_pairs={{0,96},{1,112},{16,97},{17,113},{32,0},{33,16},{48,1},{49,17},{64,... | collective-permute-start | bytes 393224 | tf_op jit(solution)/shard_map/ppermute | solution.py:282
  17.2 1.3 collective-permute-start
  18.6 3.2 %collective-permute-start.6 = (bf16[256,256]{1,0:T(8,128)(2,1)S(1)}, bf16[256,256]{1,0:T(8,128)(2,1)S(1)}, u32[]{:S(2)}, u32[]{:S(2)}) collective-permute-start(bf16[256,256]{1,0:T(8,128)(2,1)S(1)} %collective-permute-done.2.refs_0_), channel_id=1, source_target_pairs={{0,1},{1,0},{2,3},{3,2},{4,5},{5,4},{6,7},{7,6},{8,9},{9,8},{10,11... | collective-permute-start | bytes 393224 | tf_op jit(solution)/shard_map/ppermute | solution.py:269
  18.7 3.0 %collective-permute-start.7 = (bf16[256,256]{1,0:T(8,128)(2,1)S(1)}, bf16[256,256]{1,0:T(8,128)(2,1)S(1)}, u32[]{:S(2)}, u32[]{:S(2)}) collective-permute-start(bf16[256,256]{1,0:T(8,128)(2,1)S(1)} %collective-permute-done.3.refs_1_), channel_id=1, source_target_pairs={{0,1},{1,0},{2,3},{3,2},{4,5},{5,4},{6,7},{7,6},{8,9},{9,8},{10,11... | collective-permute-start | bytes 393224 | tf_op jit(solution)/shard_map/ppermute | solution.py:269
  21.2 1.3 collective-permute-start.8
  21.3 1.4 %collective-permute-start.9 = (bf16[256,256]{1,0:T(8,128)(2,1)S(1)}, bf16[256,256]{1,0:T(8,128)(2,1)S(1)}, u32[]{:S(2)}, u32[]{:S(2)}) collective-permute-start(bf16[256,256]{1,0:T(8,128)(2,1)S(1)} %collective-permute-done.5.refs_3_), channel_id=1, source_target_pairs={{0,1},{1,0},{2,3},{3,2},{4,5},{5,4},{6,7},{7,6},{8,9},{9,8},{10,11... | collective-permute-start | bytes 393224 | tf_op jit(solution)/shard_map/ppermute | solution.py:269
  26.6 7.7 %copy-start.5 = (s32[16,8]{0,1:T(8,128)S(1)}, s32[16,8]{0,1:T(8,128)}, u32[]{:S(2)}) copy-start(s32[16,8]{0,1:T(8,128)} %param.17) | copy-start | bytes 1540
  26.6 8.4 %copy-start.6 = (f32[16,8]{0,1:T(8,128)S(1)}, f32[16,8]{0,1:T(8,128)}, u32[]{:S(2)}) copy-start(f32[16,8]{0,1:T(8,128)} %param.18) | copy-start | bytes 1540
  26.6 22.3 %copy-start = (bf16[16,4096]{1,0:T(8,128)(2,1)S(1)}, bf16[16,4096]{1,0:T(8,128)(2,1)}, u32[]{:S(2)}) copy-start(bf16[16,4096]{1,0:T(8,128)(2,1)} %residual.1) | copy-start | bytes 393220
  26.6 22.3 %copy-start.3 = (f32[4096]{0:T(1024)S(1)}, f32[4096]{0:T(1024)}, u32[]{:S(2)}) copy-start(f32[4096]{0:T(1024)} %param.16) | copy-start | bytes 49156
  26.6 22.3 %all-to-all-start = ((bf16[8,16,4096]{2,1,0:T(8,128)(2,1)}), bf16[8,16,4096]{2,1,0:T(8,128)(2,1)S(1)}, u32[]{:S(2)}, u32[]{:S(2)}) async-start(bf16[8,16,4096]{2,1,0:T(8,128)(2,1)} %bitcast.13), calls=%async_computation | async-start | bytes 2097152 | tf_op jit(solution)/shard_map/all_to_all | solution.py:353
  48.9 0.7 copy-start.1
  104.8 34.9 %copy-start.2 = (s32[16,8]{1,0:T(8,128)S(1)}, s32[16,8]{1,0:T(8,128)}, u32[]{:S(2)}) copy-start(s32[16,8]{1,0:T(8,128)} %get-tuple-element.8.listed.slots) | copy-start | bytes 1540
  104.8 34.9 %copy-start.4 = (f32[16,8]{1,0:T(8,128)S(1)}, f32[16,8]{1,0:T(8,128)}, u32[]{:S(2)}) copy-start(f32[16,8]{1,0:T(8,128)} %get-tuple-element.12.weights) | copy-start | bytes 1540
